TPU v7x, 32 devices: a whole 2x2x4 slice. The times are simulated.
32 devices in a mesh: dp: 16 (over z, y, x), space: 2 (over core).
Axes of the slice: x: 2, y: 2, z: 4, core: 2. Of those that a mesh axis runs over, the one named last changes fastest.
Arguments:
- activations: bfloat16 [16, 32, 8, 256], P('dp', None, 'space'), may hold values from -6 to 6
- cotangent: bfloat16 [16, 128, 4, 64], P('dp', None, 'space'), may hold values from -12 to 12
- weight_mid: bfloat16 [3, 3, 3, 32, 64], replicated, may hold values from -0.21875 to 0.21875
- weight_deep: bfloat16 [3, 3, 3, 64, 128], replicated, may hold values from -0.15625 to 0.15625
Outputs:
- grad_input: bfloat16 [16, 32, 8, 256], P('dp', None, 'space')
- grad_mid: float32 [3, 3, 3, 32, 64], replicated
- grad_deep: float32 [3, 3, 3, 64, 128], replicated
All inputs are finite; a program needn't handle non-finite values.
Results may differ from a plain program's by a relative error of at most 0.0059.
Values may be sent and summed in bfloat16 or wider, within the bound.
A program may use at most 64 MiB of HBM per device.

v0:
```python
import jax
import jax.numpy as jnp
from jax import lax
from jax.sharding import PartitionSpec as P

ROWS = 4
COLS = 64


def extended(block, sides, width):
    for axis, dim in sides:
        count = lax.axis_size(axis)
        forward = [(i, i + 1) for i in range(count - 1)]
        backward = [(target, source) for source, target in forward]
        low = lax.ppermute(
            lax.slice_in_dim(block, block.shape[dim] - width, None, axis=dim), axis, forward
        )
        high = lax.ppermute(lax.slice_in_dim(block, 0, width, axis=dim), axis, backward)
        block = jnp.concatenate([low, block, high], axis=dim)
    return block


def shifted(planes, row_step, col_step, row_count, col_count):
    margin = col_count + 1
    widened = jnp.pad(planes, ((0, 0), (0, 0), (margin, margin)))
    offset = margin + row_step * col_count + col_step
    moved_cells = widened[:, :, offset : offset + row_count * col_count]
    column = jnp.arange(row_count * col_count) % col_count + col_step
    inside = (column >= 0) & (column < col_count)
    return jnp.where(inside, moved_cells, jnp.zeros_like(moved_cells))


def tap_patches(padded, depth_tap, row_tap, row_count, col_count):
    depth_len = padded.shape[1] - 2
    planes = padded[:, depth_tap : depth_tap + depth_len]
    stacked = jnp.stack(
        [shifted(planes, row_tap - 1, col_tap - 1, row_count, col_count) for col_tap in range(3)]
    )
    return stacked.reshape(3 * planes.shape[0], depth_len * planes.shape[2])


def conv_cube(padded, kernel, row_count, col_count):
    depth_len = padded.shape[1] - 2
    chans_in = kernel.shape[3]
    chans_out = kernel.shape[4]
    summed = jnp.zeros((chans_out, depth_len * padded.shape[2]), jnp.float32)
    for depth_tap in range(3):
        for row_tap in range(3):
            patches = tap_patches(padded, depth_tap, row_tap, row_count, col_count)
            tap_block = kernel[depth_tap, row_tap].reshape(3 * chans_in, chans_out)
            summed = summed + lax.dot_general(
                tap_block, patches, (((0,), (0,)), ((), ())), preferred_element_type=jnp.float32
            )
    return summed.reshape(chans_out, depth_len, padded.shape[2])


def weight_terms(padded, grad_out, row_count, col_count):
    chans_in = padded.shape[0]
    chans_out = grad_out.shape[0]
    flat_grad = grad_out.reshape(chans_out, -1)
    pieces = []
    for depth_tap in range(3):
        for row_tap in range(3):
            patches = tap_patches(padded, depth_tap, row_tap, row_count, col_count)
            pieces.append(
                lax.dot_general(
                    patches, flat_grad, (((1,), (1,)), ((), ())), preferred_element_type=jnp.float32
                )
            )
    return jnp.stack(pieces).reshape(3, 3, 3, chans_in, chans_out)


def flip_taps(kernel):
    return jnp.transpose(kernel[::-1, ::-1, ::-1], (0, 1, 2, 4, 3))


def pool_matrix(row_count, col_count):
    cells = jnp.arange(row_count * col_count)
    target = cells // col_count // 2 * (col_count // 2) + cells % col_count // 2
    return (target[:, None] == jnp.arange(row_count * col_count // 4)[None, :]).astype(jnp.float32)


def pool_cube(values, matrix):
    chans, depth_len, plane_len = values.shape
    paired = values.reshape(chans, depth_len // 2, 2, plane_len).sum(axis=2)
    return jnp.einsum("cdp,pq->cdq", paired, matrix, precision=lax.Precision.HIGHEST) * 0.125


def upsample_cube(values, matrix):
    spread = jnp.einsum("cdq,pq->cdp", values, matrix, precision=lax.Precision.HIGHEST)
    return jnp.repeat(spread, 2, axis=1)


def gelu_fwd(values):
    return jax.nn.gelu(values, approximate=True)


def gelu_back(pre_values, upstream):
    return jax.vjp(gelu_fwd, pre_values)[1](upstream)[0]


def extend(field, width):
    return extended(field, (("space", 1),), width)


def shards(activations, cotangent, weight_mid, weight_deep):
    row_count = ROWS
    col_count = COLS
    source = activations[0]
    matrix = pool_matrix(row_count, col_count)
    widened = extend(source, 3)
    mid_pre_wide = conv_cube(widened, weight_mid, row_count, col_count)
    pooled_wide = pool_cube(gelu_fwd(mid_pre_wide), matrix)
    position = lax.axis_index("space")
    last_index = lax.axis_size("space") - 1
    depth_ids = jnp.arange(pooled_wide.shape[1])
    outside = (depth_ids == 0) & (position == 0) | (depth_ids == pooled_wide.shape[1] - 1) & (
        position == last_index
    )
    pooled_ext = jnp.where(outside[None, :, None], 0.0, pooled_wide).astype(jnp.bfloat16)
    mid_pre = mid_pre_wide[:, 2:-2]
    source_ext = widened[:, 2:-2]
    deep_pre = conv_cube(pooled_ext, weight_deep, row_count // 2, col_count // 2)
    deep_grad = gelu_back(deep_pre, cotangent[0].astype(jnp.float32)).astype(jnp.bfloat16)
    deep_terms = weight_terms(pooled_ext, deep_grad, row_count // 2, col_count // 2)
    samples = lax.axis_size("dp")
    back_pooled = conv_cube(
        extend(deep_grad, 1), flip_taps(weight_deep), row_count // 2, col_count // 2
    )
    spread = upsample_cube(back_pooled, matrix) * 0.125
    mid_grad = gelu_back(mid_pre, spread).astype(jnp.bfloat16)
    mid_terms = weight_terms(source_ext, mid_grad, row_count, col_count)
    grad_input = conv_cube(extend(mid_grad, 1), flip_taps(weight_mid), row_count, col_count).astype(
        jnp.bfloat16
    )
    summed_mid, summed_deep = lax.psum((mid_terms, deep_terms), ("dp", "space"))
    grad_mid = summed_mid / samples
    grad_deep = summed_deep / samples
    return (grad_input[None], grad_mid, grad_deep)


def solution(mesh):
    in_specs = (P("dp", None, "space", None), P("dp", None, "space", None), P(), P())
    out_specs = (P("dp", None, "space", None), P(), P())
    return jax.shard_map(shards, mesh=mesh, in_specs=in_specs, out_specs=out_specs, check_vma=False)
```

profile of v0, /device:TPU:1, one launch (start us, length us, event | category | flops | bytes accessed | tf_op | source)
XLA Modules:
  0.0 194.0 jit_solution(2419236438906692768)
XLA Ops:
  7.2 1.0 fusion.361
  8.2 2.0 %collective-permute-start.1 = (bf16[32,3,256]{2,1,0:T(4,128)(2,1)S(1)}, bf16[32,3,256]{2,1,0:T(4,128)(2,1)S(1)}, u32[]{:S(2)}, u32[]{:S(2)}) collective-permute-start(bf16[32,3,256]{2,1,0:T(4,128)(2,1)S(1)} %get-tuple-element.193), channel_id=1, source_target_pairs={{1,0},{3,2},{5,4},{7,6},{9,8},{11,10},{13,12},{15,14},{17,16},{19,... | collective-permute-start | bytes 147464 | tf_op jit(solution)/shard_map/ppermute | solution.py:18
  10.2 1.3 collective-permute-start
  11.7 0.9 copy-done
  12.8 0.8 copy-done.1
  15.4 0.8 fusion.97
  16.4 0.4 fusion.113
  18.1 0.3 convolution_add_fusion.7
  18.4 0.3 convolution_add_fusion.6
  18.6 0.3 convolution_add_fusion.5
  18.9 0.3 convolution_add_fusion.4
  19.2 0.3 convolution_add_fusion.3
  19.5 0.3 convolution_add_fusion.2
  19.7 0.3 convolution_add_fusion.1
  20.3 0.4 reshape.331
  25.6 0.6 copy-done.5
  26.5 3.0 %collective-permute-start.3 = (bf16[128,1,64]{0,2,1:T(8,128)(2,1)S(1)}, bf16[128,1,64]{0,2,1:T(8,128)(2,1)S(1)}, u32[]{:S(2)}, u32[]{:S(2)}) collective-permute-start(bf16[128,1,64]{0,2,1:T(8,128)(2,1)S(1)} %get-tuple-element.255), channel_id=1, source_target_pairs={{1,0},{3,2},{5,4},{7,6},{9,8},{11,10},{13,12},{15,14},{17,16},{19,... | collective-permute-start | bytes 49160 | tf_op jit(solution)/shard_map/ppermute | solution.py:18
  29.5 1.5 collective-permute-start.2
  32.4 0.5 copy-done.7
  32.9 0.5 select_bitcast_fusion.6
  33.5 0.8 fusion.185
  34.2 0.3 pad_maximum_fusion.19
  34.6 0.3 pad_maximum_fusion.20
  34.9 0.3 pad_maximum_fusion.23
  35.2 0.3 pad_maximum_fusion.25
  36.2 0.6 copy-done.16
  39.8 0.6 copy-done.22
  41.1 0.6 copy-done.8
  41.7 0.4 select_bitcast_fusion.1
  42.2 3.0 %collective-permute-start.5 = (bf16[64,1,256]{2,1,0:T(2,128)(2,1)S(1)}, bf16[64,1,256]{2,1,0:T(2,128)(2,1)S(1)}, u32[]{:S(2)}, u32[]{:S(2)}) collective-permute-start(bf16[64,1,256]{2,1,0:T(2,128)(2,1)S(1)} %get-tuple-element.122), channel_id=1, source_target_pairs={{1,0},{3,2},{5,4},{7,6},{9,8},{11,10},{13,12},{15,14},{17,16},{19,... | collective-permute-start | bytes 98312 | tf_op jit(solution)/shard_map/ppermute | solution.py:18
  45.3 1.5 collective-permute-start.4
  48.7 1.0 copy.175
  49.7 0.6 copy-done.11
  50.3 1.0 select_bitcast_fusion
  51.3 1.4 fusion.49
  52.8 0.3 pad_maximum_fusion.9
  53.2 0.3 pad_maximum_fusion.10
  53.6 0.3 pad_maximum_fusion.11
  54.0 0.3 pad_maximum_fusion.12
  54.3 0.3 pad_maximum_fusion.13
  54.7 0.3 pad_maximum_fusion.14
  55.1 0.3 pad_maximum_fusion.15
  55.5 0.3 pad_maximum_fusion.16
  57.2 0.3 pad_maximum_fusion.17
  58.0 0.7 convert_element_type.219
  58.7 125.6 %all-reduce.18.cloned.1.call-done = (f32[3,3,3,32,64]{4,3,2,1,0:T(8,128)}, f32[3,3,3,64,128]{4,3,2,1,0:T(8,128)}) async-done(((f32[3,3,3,32,64]{4,3,2,1,0:T(8,128)}, f32[3,3,3,64,128]{4,3,2,1,0:T(8,128)}), (f32[3,3,3,32,64]{4,3,2,1,0:T(8,128)}, f32[3,3,3,64,128]{4,3,2,1,0:T(8,128)})) %all-reduce.18.cloned.1.call-update) | async-done | bytes 1105936 | tf_op jit(solution)/shard_map/psum | solution.py:136
  184.3 1.9 broadcast_multiply_fusion.1
  186.1 1.0 broadcast_multiply_fusion
  (232 shorter events, 17.9 us)
Async XLA Ops:
  7.2 4.4 %copy-start.4 = (bf16[3,3,3,32,64]{4,3,2,1,0:T(8,128)(2,1)S(1)}, bf16[3,3,3,32,64]{4,3,2,1,0:T(8,128)(2,1)}, u32[]{:S(2)}) copy-start(bf16[3,3,3,32,64]{4,3,2,1,0:T(8,128)(2,1)} %param.6) | copy-start | bytes 331780
  7.2 177.1 %all-reduce.18.cloned.1.call-start = ((), (), s32[]{:S(2)}) async-start(), calls=%async_computation | async-start | bytes 2654208 | tf_op jit(solution)/shard_map/psum | solution.py:136
  8.2 6.9 %collective-permute-start.1 = (bf16[32,3,256]{2,1,0:T(4,128)(2,1)S(1)}, bf16[32,3,256]{2,1,0:T(4,128)(2,1)S(1)}, u32[]{:S(2)}, u32[]{:S(2)}) collective-permute-start(bf16[32,3,256]{2,1,0:T(4,128)(2,1)S(1)} %get-tuple-element.193), channel_id=1, source_target_pairs={{1,0},{3,2},{5,4},{7,6},{9,8},{11,10},{13,12},{15,14},{17,16},{19,... | collective-permute-start | bytes 147464 | tf_op jit(solution)/shard_map/ppermute | solution.py:18
  10.2 5.0 %collective-permute-start = (bf16[32,3,256]{2,1,0:T(4,128)(2,1)S(1)}, bf16[32,3,256]{2,1,0:T(4,128)(2,1)S(1)}, u32[]{:S(2)}, u32[]{:S(2)}) collective-permute-start(bf16[32,3,256]{2,1,0:T(4,128)(2,1)S(1)} %get-tuple-element.192), channel_id=1, source_target_pairs={{0,1},{2,3},{4,5},{6,7},{8,9},{10,11},{12,13},{14,15},{16,17},{18,... | collective-permute-start | bytes 147464 | tf_op jit(solution)/shard_map/ppermute | solution.py:15
  11.5 4.9 %copy-start.6 = (pred[256]{0:T(512)(128)(4,1)}, pred[256]{0:T(512)(128)(4,1)S(1)}, u32[]{:S(2)}) copy-start(pred[256]{0:T(512)(128)(4,1)S(1)} %compare_and_fusion.3) | copy-start | bytes 772
  11.5 10.8 %copy-start.17 = (pred[64]{0:T(512)(128)(4,1)}, pred[64]{0:T(512)(128)(4,1)S(1)}, u32[]{:S(2)}) copy-start(pred[64]{0:T(512)(128)(4,1)S(1)} %get-tuple-element.327) | copy-start | bytes 196
  11.5 19.5 %copy-start.15 = (pred[64]{0:T(512)(128)(4,1)}, pred[64]{0:T(512)(128)(4,1)S(1)}, u32[]{:S(2)}) copy-start(pred[64]{0:T(512)(128)(4,1)S(1)} %get-tuple-element.328) | copy-start | bytes 196
  11.5 4.8 %copy-start.9 = (pred[256]{0:T(512)(128)(4,1)}, pred[256]{0:T(512)(128)(4,1)S(1)}, u32[]{:S(2)}) copy-start(pred[256]{0:T(512)(128)(4,1)S(1)} %compare_and_fusion.5) | copy-start | bytes 772
  11.6 4.8 %copy-start.12 = (pred[256]{0:T(512)(128)(4,1)}, pred[256]{0:T(512)(128)(4,1)S(1)}, u32[]{:S(2)}) copy-start(pred[256]{0:T(512)(128)(4,1)S(1)} %compare_and_fusion.2) | copy-start | bytes 772
  11.6 1.0 copy-start
  11.7 9.3 %copy-start.21 = (s32[256]{0:T(256)}, s32[256]{0:T(256)S(1)}, u32[]{:S(2)}) copy-start(s32[256]{0:T(256)S(1)} %fusion.353) | copy-start | bytes 3076
  12.6 9.7 %copy-start.19 = (pred[64]{0:T(512)(128)(4,1)}, pred[64]{0:T(512)(128)(4,1)S(1)}, u32[]{:S(2)}) copy-start(pred[64]{0:T(512)(128)(4,1)S(1)} %compare_and_fusion.4) | copy-start | bytes 196
  12.7 0.8 copy-start.1
  25.4 0.8 copy-start.5
  26.5 9.7 %collective-permute-start.3 = (bf16[128,1,64]{0,2,1:T(8,128)(2,1)S(1)}, bf16[128,1,64]{0,2,1:T(8,128)(2,1)S(1)}, u32[]{:S(2)}, u32[]{:S(2)}) collective-permute-start(bf16[128,1,64]{0,2,1:T(8,128)(2,1)S(1)} %get-tuple-element.255), channel_id=1, source_target_pairs={{1,0},{3,2},{5,4},{7,6},{9,8},{11,10},{13,12},{15,14},{17,16},{19,... | collective-permute-start | bytes 49160 | tf_op jit(solution)/shard_map/ppermute | solution.py:18
  29.5 6.7 %collective-permute-start.2 = (bf16[128,1,64]{0,2,1:T(8,128)(2,1)S(1)}, bf16[128,1,64]{0,2,1:T(8,128)(2,1)S(1)}, u32[]{:S(2)}, u32[]{:S(2)}) collective-permute-start(bf16[128,1,64]{0,2,1:T(8,128)(2,1)S(1)} %get-tuple-element.256), channel_id=1, source_target_pairs={{0,1},{2,3},{4,5},{6,7},{8,9},{10,11},{12,13},{14,15},{16,17},{18,... | collective-permute-start | bytes 49160 | tf_op jit(solution)/shard_map/ppermute | solution.py:15
  32.2 0.7 copy-start.7
  32.2 0.7 copy-start.10
  32.3 0.7 copy-start.13
  32.9 1.3 copy-start.2
  36.2 0.7 copy-start.16
  36.2 0.7 copy-start.18
  36.2 0.7 copy-start.20
  39.7 0.7 copy-start.22
  41.0 0.7 copy-start.8
  42.2 7.4 %collective-permute-start.5 = (bf16[64,1,256]{2,1,0:T(2,128)(2,1)S(1)}, bf16[64,1,256]{2,1,0:T(2,128)(2,1)S(1)}, u32[]{:S(2)}, u32[]{:S(2)}) collective-permute-start(bf16[64,1,256]{2,1,0:T(2,128)(2,1)S(1)} %get-tuple-element.122), channel_id=1, source_target_pairs={{1,0},{3,2},{5,4},{7,6},{9,8},{11,10},{13,12},{15,14},{17,16},{19,... | collective-permute-start | bytes 98312 | tf_op jit(solution)/shard_map/ppermute | solution.py:18
  45.3 4.4 %collective-permute-start.4 = (bf16[64,1,256]{2,1,0:T(2,128)(2,1)S(1)}, bf16[64,1,256]{2,1,0:T(2,128)(2,1)S(1)}, u32[]{:S(2)}, u32[]{:S(2)}) collective-permute-start(bf16[64,1,256]{2,1,0:T(2,128)(2,1)S(1)} %get-tuple-element.123), channel_id=1, source_target_pairs={{0,1},{2,3},{4,5},{6,7},{8,9},{10,11},{12,13},{14,15},{16,17},{18,... | collective-permute-start | bytes 98312 | tf_op jit(solution)/shard_map/ppermute | solution.py:15
  49.6 0.7 copy-start.11
  49.6 0.7 copy-start.14
  184.3 1.9 copy-start.3
Sparse Core Ops, SparseCore 0:
  49.8 134.4 all-reduce.17
where the time goes:
time: 195 us; the launch traced here: 194 us
  waiting for transfers between devices  126 us (65%)
  between operations  15.6 us (8%)
  local copies, waits for them, and re-layouts  14.8 us (8%)
  other arithmetic  14.8 us (8%)
  starting transfers between devices  12.3 us (6%)
  matrix products  10.9 us (6%)
    psum x1, waiting for transfers between devices, shards(): summed_mid, summed_deep = lax.psum((mid_terms, deep_terms), ('dp', 'space'))  126 us
    another operation x50, other arithmetic, tap_patches(): jnp.stack([shifted(planes, row_tap - 1, col_tap - 1, row_count, col_count...  11.3 us
    ppermute x3, starting transfers between devices, extended(): lax.ppermute(lax.slice_in_dim(block, 0, width, axis=dim), axis, backward)  8.03 us
    dot_general x36, matrix products, conv_cube(): lax.dot_general(tap_block, patches, (((0,), (0,)), ((), ())), preferred_e...  7.42 us
    unnamed x75, local copies, waits for them, and re-layouts  6.88 us
    ppermute x3, starting transfers between devices, extended(): lax.ppermute(lax.slice_in_dim(block, block.shape[dim] - width, None, axis...  4.28 us
  transfers between devices with their start and end apart: 7, of which 1 were waited for; matrix products, arithmetic and copies ran while one was open for 9% of the time, Pallas kernels for 0%

commit v1 on v0

--- a/solution.py
+++ b/solution.py
@@ -1,11 +1,189 @@
+import functools
+
 import jax
 import jax.numpy as jnp
 from jax import lax
+from jax.experimental import pallas as pl
+from jax.experimental.pallas import tpu as pltpu
 from jax.sharding import PartitionSpec as P
 
 ROWS = 4
 COLS = 64
-
+LANES = 128
+ROW_TILE = 16
+
+
+def group_stages(samples, slabs):
+    stages = [("space", slabs, 1)]
+    stride = 1
+    for size in (2, 2, 4):
+        if samples // stride % size == 0:
+            stages.append(("dp", size, stride))
+            stride *= size
+    if samples // stride > 1:
+        stages.append(("dp", samples // stride, stride))
+    return stages
+
+
+def place(axis, size, stride):
+    return lax.rem(lax.axis_index(axis) // stride, size)
+
+
+def partner(axis, size, stride, step):
+    own = place(axis, size, stride)
+    other = lax.rem(own + step, size)
+    dp, space = lax.axis_index("dp"), lax.axis_index("space")
+    if axis == "space":
+        return other, (dp, other)
+    return other, (dp + (other - own) * stride, space)
+
+
+def rows_at(start, count):
+    return pl.ds(pl.multiple_of(start, ROW_TILE), count)
+
+
+class Reduction:
+    def __init__(self, stages, total, outgoing, gathered, landing, sems):
+        self.stages, self.total, self.outgoing = stages, total, outgoing
+        self.gathered, self.landing, self.sems = gathered, landing, sems
+        self.start, self.length = 0, total.shape[0]
+        self.starts, self.copies, self.sent, self.used = [], [], [], 0
+
+    def copy(self, source, target, device):
+        send, recv = self.sems
+        made = pltpu.make_async_remote_copy(
+            src_ref=source,
+            dst_ref=target,
+            send_sem=send.at[self.used],
+            recv_sem=recv.at[self.used],
+            device_id=device,
+            device_id_type=pl.DeviceIdType.MESH,
+        )
+        self.used += 1
+        made.start()
+        self.copies.append(made)
+
+    def scatter_start(self, index):
+        axis, size, stride = self.stages[index]
+        piece = self.length // size
+        for step in range(1, size):
+            other, device = partner(axis, size, stride, step)
+            window = rows_at(self.start + other * piece, piece)
+            self.outgoing[window] = self.total[window].astype(jnp.bfloat16)
+            self.copy(self.outgoing.at[window], self.landing[index].at[step - 1], device)
+        self.starts.append(self.start)
+        self.start = self.start + place(axis, size, stride) * piece
+        self.length = piece
+
+    def scatter_finish(self, index):
+        window = rows_at(self.start, self.length)
+        value = self.total[window]
+        for step, made in enumerate(self.copies):
+            made.wait_recv()
+            value = value + self.landing[index][step].astype(jnp.float32)
+        self.total[window] = value
+        self.sent += self.copies
+        self.copies = []
+
+    def gather_own(self):
+        window = rows_at(self.start, self.length)
+        self.gathered[window] = self.total[window].astype(jnp.bfloat16)
+
+    def gather_start(self, index):
+        axis, size, stride = self.stages[index]
+        window = rows_at(self.start, self.length)
+        for step in range(1, size):
+            _, device = partner(axis, size, stride, step)
+            self.copy(self.gathered.at[window], self.gathered.at[window], device)
+        self.start = self.starts[index]
+        self.length = self.length * size
+
+    def gather_finish(self):
+        for made in self.copies:
+            made.wait_recv()
+        self.sent += self.copies
+        self.copies = []
+
+    def drain(self):
+        for made in self.sent:
+            made.wait_send()
+
+
+def reduction_rows(rows, devices):
+    return -(-rows // (devices * ROW_TILE)) * ROW_TILE * devices
+
+
+def reduction_scratch(stages, rows):
+    shapes = [
+        pltpu.VMEM((rows, LANES), jnp.float32),
+        pltpu.VMEM((rows, LANES), jnp.bfloat16),
+        pltpu.VMEM((rows, LANES), jnp.bfloat16),
+    ]
+    length, count = rows, 0
+    for _, size, _ in stages:
+        length //= size
+        count += 2 * (size - 1)
+        shapes.append(pltpu.VMEM((size - 1, length, LANES), jnp.bfloat16))
+    return shapes + [pltpu.SemaphoreType.DMA((count,)), pltpu.SemaphoreType.DMA((count,))]
+
+
+def greet(stages):
+    barrier = pltpu.get_barrier_semaphore()
+    count = 0
+    for axis, size, stride in stages:
+        for step in range(1, size):
+            _, device = partner(axis, size, stride, step)
+            pl.semaphore_signal(barrier, inc=1, device_id=device, device_id_type=pl.DeviceIdType.MESH)
+            count += 1
+    pl.semaphore_wait(barrier, count)
+
+
+def sum_kernel(stages, scale, mid_ref, deep_ref, mid_out, deep_out, total, outgoing, gathered, *rest):
+    half = mid_ref.shape[0] // 2
+    wide = mid_ref.shape[1]
+    deep_rows = deep_ref.shape[0]
+    used = deep_rows + half
+    total[:deep_rows] = deep_ref[...]
+    total[deep_rows:used, :wide] = mid_ref[:half]
+    total[deep_rows:used, wide:] = mid_ref[half:]
+    if used < total.shape[0]:
+        total[used:] = jnp.zeros((total.shape[0] - used, LANES), jnp.float32)
+    greet(stages)
+    work = Reduction(stages, total, outgoing, gathered, rest[: len(stages)], rest[len(stages) :])
+    for index in range(len(stages)):
+        work.scatter_start(index)
+        work.scatter_finish(index)
+    work.gather_own()
+    for index in reversed(range(len(stages))):
+        work.gather_start(index)
+        work.gather_finish()
+    deep_out[...] = gathered[:deep_rows].astype(jnp.float32) * scale
+    packed = gathered[deep_rows:used].astype(jnp.float32) * scale
+    mid_out[:half] = packed[:, :wide]
+    mid_out[half:] = packed[:, wide:]
+    work.drain()
+
+
+def summed_terms(mid_terms, deep_terms):
+    samples, slabs = lax.axis_size("dp"), lax.axis_size("space")
+    stages = group_stages(samples, slabs)
+    mid_flat = mid_terms.reshape(-1, mid_terms.shape[-1])
+    deep_flat = deep_terms.reshape(-1, LANES)
+    rows = reduction_rows(deep_flat.shape[0] + mid_flat.shape[0] // 2, samples * slabs)
+    mid_sum, deep_sum = pl.pallas_call(
+        functools.partial(sum_kernel, stages, 1.0 / samples),
+        out_shape=[
+            jax.ShapeDtypeStruct(mid_flat.shape, jnp.float32),
+            jax.ShapeDtypeStruct(deep_flat.shape, jnp.float32),
+        ],
+        in_specs=[pl.BlockSpec(memory_space=pltpu.VMEM)] * 2,
+        out_specs=[pl.BlockSpec(memory_space=pltpu.VMEM)] * 2,
+        scratch_shapes=reduction_scratch(stages, rows),
+        compiler_params=pltpu.CompilerParams(
+            collective_id=0, has_side_effects=True, vmem_limit_bytes=48 * 1024 * 1024
+        ),
+    )(mid_flat, deep_flat)
+    return mid_sum.reshape(mid_terms.shape), deep_sum.reshape(deep_terms.shape)
 
 def extended(block, sides, width):
     for axis, dim in sides:
@@ -123,7 +301,6 @@
     deep_pre = conv_cube(pooled_ext, weight_deep, row_count // 2, col_count // 2)
     deep_grad = gelu_back(deep_pre, cotangent[0].astype(jnp.float32)).astype(jnp.bfloat16)
     deep_terms = weight_terms(pooled_ext, deep_grad, row_count // 2, col_count // 2)
-    samples = lax.axis_size("dp")
     back_pooled = conv_cube(
         extend(deep_grad, 1), flip_taps(weight_deep), row_count // 2, col_count // 2
     )
@@ -133,9 +310,7 @@
     grad_input = conv_cube(extend(mid_grad, 1), flip_taps(weight_mid), row_count, col_count).astype(
         jnp.bfloat16
     )
-    summed_mid, summed_deep = lax.psum((mid_terms, deep_terms), ("dp", "space"))
-    grad_mid = summed_mid / samples
-    grad_deep = summed_deep / samples
+    grad_mid, grad_deep = summed_terms(mid_terms, deep_terms)
     return (grad_input[None], grad_mid, grad_deep)
 
 

time: 195 us -> 109 us (0.56)
  waiting for transfers between devices: 126 us -> 0.02 us
  Pallas kernels: 0 us -> 33.6 us
  local copies, waits for them, and re-layouts: 14.8 us -> 35.8 us
  between operations: 15.6 us -> 2.12 us
  other arithmetic: 14.8 us -> 12.8 us
    psum x1 -> x0, waiting for transfers between devices: 126 us -> none  [shards(): summed_mid, summed_deep = lax.psum((mid_terms, deep_terms), ('dp', 'space'))]
    pallas_call x0 -> x1, Pallas kernels: none -> 33.6 us  [summed_terms(): pl.pallas_call(functools.partial(sum_kernel, stages, 1.0 / samples), out_...]
    unnamed x75 -> x103, local copies, waits for them, and re-layouts: 6.88 us -> 20.1 us
    slice x22, local copies, waits for them, and re-layouts: 0.67 us -> 5.03 us  [conv_cube(): tap_block = kernel[depth_tap, row_tap].reshape(3 * chans_in, chans_out)]
    another operation x9, local copies, waits for them, and re-layouts: 0.86 us -> 4.43 us  [conv_cube(): tap_block = kernel[depth_tap, row_tap].reshape(3 * chans_in, chans_out)]
    div x2 -> x0, other arithmetic: 2.89 us -> none  [the longest x1 1.89 us: shards(): grad_mid = summed_mid / samples]
  transfers between devices with their start and end apart: 7 -> 6, of which waited for: 1 -> 0; matrix products, arithmetic and copies ran while one was open for 9% -> 17% of each run, Pallas kernels for 0% -> 31%
where the time goes in v1:
time: 109 us; the launch traced here: 108 us
  local copies, waits for them, and re-layouts  35.8 us (33%)
  Pallas kernels  33.6 us (31%)
  starting transfers between devices  13 us (12%)
  other arithmetic  12.8 us (12%)
  matrix products  10.8 us (10%)
  between operations  2.12 us (2%)
    pallas_call x1, Pallas kernels, summed_terms(): pl.pallas_call(functools.partial(sum_kernel, stages, 1.0 / samples), out_...  33.6 us
    unnamed x103, local copies, waits for them, and re-layouts  20.1 us
    another operation x50, other arithmetic, tap_patches(): jnp.stack([shifted(planes, row_tap - 1, col_tap - 1, row_count, col_count...  12.1 us
    ppermute x3, starting transfers between devices, extended(): lax.ppermute(lax.slice_in_dim(block, 0, width, axis=dim), axis, backward)  8.76 us
    dot_general x36, matrix products, conv_cube(): lax.dot_general(tap_block, patches, (((0,), (0,)), ((), ())), preferred_e...  7.35 us
    slice x22, local copies, waits for them, and re-layouts, conv_cube(): tap_block = kernel[depth_tap, row_tap].reshape(3 * chans_in, chans_out)  5.03 us
    another operation x9, local copies, waits for them, and re-layouts, conv_cube(): tap_block = kernel[depth_tap, row_tap].reshape(3 * chans_in, chans_out)  4.43 us
    ppermute x3, starting transfers between devices, extended(): lax.ppermute(lax.slice_in_dim(block, block.shape[dim] - width, None, axis...  4.27 us
  transfers between devices with their start and end apart: 6, of which 0 were waited for; matrix products, arithmetic and copies ran while one was open for 17% of the time, Pallas kernels for 31%

profile of v1, /device:TPU:1, one launch (start us, length us, event | category | flops | bytes accessed | tf_op | source)
XLA Modules:
  0.0 108.2 jit_solution(16980151389939771317)
XLA Ops:
  0.6 1.0 fusion.361
  1.6 2.0 %collective-permute-start.1 = (bf16[32,3,256]{2,1,0:T(4,128)(2,1)S(1)}, bf16[32,3,256]{2,1,0:T(4,128)(2,1)S(1)}, u32[]{:S(2)}, u32[]{:S(2)}) collective-permute-start(bf16[32,3,256]{2,1,0:T(4,128)(2,1)S(1)} %get-tuple-element.195), channel_id=1, source_target_pairs={{1,0},{3,2},{5,4},{7,6},{9,8},{11,10},{13,12},{15,14},{17,16},{19,... | collective-permute-start | bytes 147464 | tf_op jit(solution)/shard_map/ppermute | solution.py:196
  3.6 1.3 %collective-permute-start = (bf16[32,3,256]{2,1,0:T(4,128)(2,1)S(1)}, bf16[32,3,256]{2,1,0:T(4,128)(2,1)S(1)}, u32[]{:S(2)}, u32[]{:S(2)}) collective-permute-start(bf16[32,3,256]{2,1,0:T(4,128)(2,1)S(1)} %get-tuple-element.194), channel_id=1, source_target_pairs={{0,1},{2,3},{4,5},{6,7},{8,9},{10,11},{12,13},{14,15},{16,17},{18,... | collective-permute-start | bytes 147464 | tf_op jit(solution)/shard_map/ppermute | solution.py:193
  5.1 0.9 copy-done
  6.2 0.8 copy-done.1
  7.2 0.7 copy.149
  7.9 0.7 copy.151
  8.5 0.7 copy.153
  9.2 0.7 copy.155
  9.9 0.7 copy.157
  10.5 0.7 copy.159
  11.2 0.7 copy.161
  12.1 0.7 reshape_squeeze.137
  12.8 0.7 reshape_squeeze.138
  13.5 0.7 reshape_squeeze.139
  14.2 0.7 reshape_squeeze.140
  14.9 0.7 reshape_squeeze.141
  15.6 0.7 reshape_squeeze.142
  16.7 0.8 fusion.97
  26.9 0.6 copy-done.14
  27.7 3.0 %collective-permute-start.3 = (bf16[128,1,64]{0,2,1:T(8,128)(2,1)S(1)}, bf16[128,1,64]{0,2,1:T(8,128)(2,1)S(1)}, u32[]{:S(2)}, u32[]{:S(2)}) collective-permute-start(bf16[128,1,64]{0,2,1:T(8,128)(2,1)S(1)} %get-tuple-element.257), channel_id=1, source_target_pairs={{1,0},{3,2},{5,4},{7,6},{9,8},{11,10},{13,12},{15,14},{17,16},{19,... | collective-permute-start | bytes 49160 | tf_op jit(solution)/shard_map/ppermute | solution.py:196
  30.8 1.5 %collective-permute-start.2 = (bf16[128,1,64]{0,2,1:T(8,128)(2,1)S(1)}, bf16[128,1,64]{0,2,1:T(8,128)(2,1)S(1)}, u32[]{:S(2)}, u32[]{:S(2)}) collective-permute-start(bf16[128,1,64]{0,2,1:T(8,128)(2,1)S(1)} %get-tuple-element.258), channel_id=1, source_target_pairs={{0,1},{2,3},{4,5},{6,7},{8,9},{10,11},{12,13},{14,15},{16,17},{18,... | collective-permute-start | bytes 49160 | tf_op jit(solution)/shard_map/ppermute | solution.py:193
  33.6 0.6 select_bitcast_fusion.6
  34.2 0.8 fusion.185
  36.7 0.7 copy.214
  37.4 0.7 copy.216
  38.1 0.7 copy.217
  38.8 0.7 copy.218
  41.8 0.7 copy-done.13
  42.6 0.7 copy-done.12
  43.4 0.7 copy-done.11
  44.3 0.7 copy-done.10
  45.1 0.7 copy-done.9
  45.9 0.7 copy-done.8
  46.8 0.7 copy-done.7
  49.1 0.7 copy-done.22
  50.2 0.7 fusion.360
  51.0 3.8 %collective-permute-start.5 = (bf16[64,1,256]{2,1,0:T(2,128)(2,1)}, bf16[64,1,256]{2,1,0:T(2,128)(2,1)}, u32[]{:S(2)}, u32[]{:S(2)}) collective-permute-start(bf16[64,1,256]{2,1,0:T(2,128)(2,1)} %get-tuple-element.124), channel_id=1, source_target_pairs={{1,0},{3,2},{5,4},{7,6},{9,8},{11,10},{13,12},{15,14},{17,16},{19,... | collective-permute-start | bytes 98312 | tf_op jit(solution)/shard_map/ppermute | solution.py:196
  54.7 1.5 %collective-permute-start.4 = (bf16[64,1,256]{2,1,0:T(2,128)(2,1)}, bf16[64,1,256]{2,1,0:T(2,128)(2,1)}, u32[]{:S(2)}, u32[]{:S(2)}) collective-permute-start(bf16[64,1,256]{2,1,0:T(2,128)(2,1)} %get-tuple-element.125), channel_id=1, source_target_pairs={{0,1},{2,3},{4,5},{6,7},{8,9},{10,11},{12,13},{14,15},{16,17},{18,... | collective-permute-start | bytes 98312 | tf_op jit(solution)/shard_map/ppermute | solution.py:193
  56.5 0.7 copy-done.4
  57.6 0.7 copy-done.6
  59.7 33.6 %shard_map.67 = (f32[864,64]{1,0:T(8,128)S(1)}, f32[1728,128]{1,0:T(8,128)S(1)}) custom-call(f32[864,64]{1,0:T(8,128)S(1)} %bitcast.735, f32[1728,128]{1,0:T(8,128)S(1)} %bitcast.736), custom_call_target="tpu_custom_call" | custom-call | tf_op jit(solution)/shard_map/pallas_call | solution.py:173
  93.4 0.6 copy-done.23
  94.1 1.9 %select_bitcast_fusion = (bf16[1,64,4,256]{3,2,1,0:T(4,128)(2,1)S(1)}, bf16[64,4,256]{2,1,0:T(4,128)(2,1)S(1)}, bf16[1,64,4,256]{3,2,1,0:T(4,128)(2,1)S(1)}, bf1...) fusion(pred[256]{0:T(512)(128)(4,1)S(1)} %copy-done.23, ...), kind=kLoop, calls=%fused_computation.317 | loop fusion | flops 1179648 | bytes 1770240 | tf_op jit(solution)/shard_map/stack | solution.py:214
  96.0 1.4 %fusion.49 = (bf16[1,64,4,256]{3,2,1,0:T(4,128)(2,1)S(1)}, bf16[1,64,4,256]{3,2,1,0:T(4,128)(2,1)S(1)}, bf16[1,64,4,256]{3,2,1,0:T(4,128)(2,1)S(1)}, bf16[1,64,4...) fusion(bf16[64,4,256]{2,1,0:T(4,128)(2,1)S(1)} %get-tuple-eleme, ...), kind=kLoop, calls=%fused_computation.230 | loop fusion | flops 1048576 | bytes 2360064 | tf_op jit(solution)/shard_map/stack | solution.py:214
  105.8 0.7 convert_element_type.219
  106.5 0.8 copy.317
  107.3 0.9 copy.318
  (256 shorter events, 28.6 us)
Async XLA Ops:
  0.6 4.4 %copy-start.2 = (bf16[3,3,3,32,64]{4,3,2,1,0:T(8,128)(2,1)S(1)}, bf16[3,3,3,32,64]{4,3,2,1,0:T(8,128)(2,1)}, u32[]{:S(2)}) copy-start(bf16[3,3,3,32,64]{4,3,2,1,0:T(8,128)(2,1)} %param.6) | copy-start | bytes 331780
  1.6 14.8 %collective-permute-start.1 = (bf16[32,3,256]{2,1,0:T(4,128)(2,1)S(1)}, bf16[32,3,256]{2,1,0:T(4,128)(2,1)S(1)}, u32[]{:S(2)}, u32[]{:S(2)}) collective-permute-start(bf16[32,3,256]{2,1,0:T(4,128)(2,1)S(1)} %get-tuple-element.195), channel_id=1, source_target_pairs={{1,0},{3,2},{5,4},{7,6},{9,8},{11,10},{13,12},{15,14},{17,16},{19,... | collective-permute-start | bytes 147464 | tf_op jit(solution)/shard_map/ppermute | solution.py:196
  3.6 12.8 %collective-permute-start = (bf16[32,3,256]{2,1,0:T(4,128)(2,1)S(1)}, bf16[32,3,256]{2,1,0:T(4,128)(2,1)S(1)}, u32[]{:S(2)}, u32[]{:S(2)}) collective-permute-start(bf16[32,3,256]{2,1,0:T(4,128)(2,1)S(1)} %get-tuple-element.194), channel_id=1, source_target_pairs={{0,1},{2,3},{4,5},{6,7},{8,9},{10,11},{12,13},{14,15},{16,17},{18,... | collective-permute-start | bytes 147464 | tf_op jit(solution)/shard_map/ppermute | solution.py:193
  4.9 29.3 %copy-start.21 = (pred[256]{0:T(512)(128)(4,1)}, pred[256]{0:T(512)(128)(4,1)S(1)}, u32[]{:S(2)}) copy-start(pred[256]{0:T(512)(128)(4,1)S(1)} %compare_and_fusion.3) | copy-start | bytes 772
  4.9 18.6 %copy-start.30 = (pred[64]{0:T(512)(128)(4,1)}, pred[64]{0:T(512)(128)(4,1)S(1)}, u32[]{:S(2)}) copy-start(pred[64]{0:T(512)(128)(4,1)S(1)} %get-tuple-element.329) | copy-start | bytes 196
  4.9 27.3 %copy-start.28 = (pred[64]{0:T(512)(128)(4,1)}, pred[64]{0:T(512)(128)(4,1)S(1)}, u32[]{:S(2)}) copy-start(pred[64]{0:T(512)(128)(4,1)S(1)} %get-tuple-element.330) | copy-start | bytes 196
  5.0 29.2 %copy-start.24 = (pred[256]{0:T(512)(128)(4,1)}, pred[256]{0:T(512)(128)(4,1)S(1)}, u32[]{:S(2)}) copy-start(pred[256]{0:T(512)(128)(4,1)S(1)} %compare_and_fusion.5) | copy-start | bytes 772
  5.0 29.2 %copy-start.26 = (pred[256]{0:T(512)(128)(4,1)}, pred[256]{0:T(512)(128)(4,1)S(1)}, u32[]{:S(2)}) copy-start(pred[256]{0:T(512)(128)(4,1)S(1)} %compare_and_fusion.2) | copy-start | bytes 772
  5.0 1.0 copy-start
  5.1 17.2 %copy-start.34 = (s32[256]{0:T(256)}, s32[256]{0:T(256)S(1)}, u32[]{:S(2)}) copy-start(s32[256]{0:T(256)S(1)} %fusion.353) | copy-start | bytes 3076
  6.0 17.6 %copy-start.32 = (pred[64]{0:T(512)(128)(4,1)}, pred[64]{0:T(512)(128)(4,1)S(1)}, u32[]{:S(2)}) copy-start(pred[64]{0:T(512)(128)(4,1)S(1)} %compare_and_fusion.4) | copy-start | bytes 196
  6.1 0.8 copy-start.1
  26.7 0.8 copy-start.14
  27.7 11.9 %collective-permute-start.3 = (bf16[128,1,64]{0,2,1:T(8,128)(2,1)S(1)}, bf16[128,1,64]{0,2,1:T(8,128)(2,1)S(1)}, u32[]{:S(2)}, u32[]{:S(2)}) collective-permute-start(bf16[128,1,64]{0,2,1:T(8,128)(2,1)S(1)} %get-tuple-element.257), channel_id=1, source_target_pairs={{1,0},{3,2},{5,4},{7,6},{9,8},{11,10},{13,12},{15,14},{17,16},{19,... | collective-permute-start | bytes 49160 | tf_op jit(solution)/shard_map/ppermute | solution.py:196
  30.8 8.9 %collective-permute-start.2 = (bf16[128,1,64]{0,2,1:T(8,128)(2,1)S(1)}, bf16[128,1,64]{0,2,1:T(8,128)(2,1)S(1)}, u32[]{:S(2)}, u32[]{:S(2)}) collective-permute-start(bf16[128,1,64]{0,2,1:T(8,128)(2,1)S(1)} %get-tuple-element.258), channel_id=1, source_target_pairs={{0,1},{2,3},{4,5},{6,7},{8,9},{10,11},{12,13},{14,15},{16,17},{18,... | collective-permute-start | bytes 49160 | tf_op jit(solution)/shard_map/ppermute | solution.py:193
  39.6 0.6 copy-start.29
  39.6 0.6 copy-start.31
  39.6 0.6 copy-start.33
  41.6 0.8 copy-start.13
  42.4 0.8 copy-start.12
  43.3 0.8 copy-start.11
  44.1 0.8 copy-start.10
  44.9 0.8 copy-start.9
  45.8 0.8 copy-start.8
  46.6 0.8 copy-start.7
  47.8 0.7 copy-start.35
  49.1 0.7 copy-start.22
  51.0 5.3 %copy-start.3 = (bf16[12,8,4,256]{3,1,2,0:T(8,128)(2,1)S(1)}, bf16[12,8,4,256]{3,1,2,0:T(8,128)(2,1)}, u32[]{:S(2)}) copy-start(bf16[12,8,4,256]{3,1,2,0:T(8,128)(2,1)} %copy.214) | copy-start | bytes 589828
  51.0 42.5 %collective-permute-start.5 = (bf16[64,1,256]{2,1,0:T(2,128)(2,1)}, bf16[64,1,256]{2,1,0:T(2,128)(2,1)}, u32[]{:S(2)}, u32[]{:S(2)}) collective-permute-start(bf16[64,1,256]{2,1,0:T(2,128)(2,1)} %get-tuple-element.124), channel_id=1, source_target_pairs={{1,0},{3,2},{5,4},{7,6},{9,8},{11,10},{13,12},{15,14},{17,16},{19,... | collective-permute-start | bytes 98312 | tf_op jit(solution)/shard_map/ppermute | solution.py:196
  54.7 38.7 %collective-permute-start.4 = (bf16[64,1,256]{2,1,0:T(2,128)(2,1)}, bf16[64,1,256]{2,1,0:T(2,128)(2,1)}, u32[]{:S(2)}, u32[]{:S(2)}) collective-permute-start(bf16[64,1,256]{2,1,0:T(2,128)(2,1)} %get-tuple-element.125), channel_id=1, source_target_pairs={{0,1},{2,3},{4,5},{6,7},{8,9},{10,11},{12,13},{14,15},{16,17},{18,... | collective-permute-start | bytes 98312 | tf_op jit(solution)/shard_map/ppermute | solution.py:193
  56.3 0.9 copy-start.4
  56.5 1.0 copy-start.5
  57.4 0.9 copy-start.6
  93.4 0.7 copy-start.23
  93.4 0.7 copy-start.25
  93.4 0.7 copy-start.27
  101.2 0.7 copy-start.15
  101.9 0.7 copy-start.16
  102.6 0.7 copy-start.17
  103.3 0.7 copy-start.18
  104.0 0.7 copy-start.19
  104.8 0.7 copy-start.20

commit v2 on v1

v2 whole, which is shorter than its diff:
```python
import functools

import jax
import jax.numpy as jnp
from jax import lax
from jax.experimental import pallas as pl
from jax.experimental.pallas import tpu as pltpu
from jax.sharding import PartitionSpec as P

ROWS = 4
COLS = 64
LANES = 128
ROW_TILE = 16


def group_stages(samples, slabs):
    stages = [("space", slabs, 1)]
    stride = 1
    for size in (2, 2, 4):
        if samples // stride % size == 0:
            stages.append(("dp", size, stride))
            stride *= size
    if samples // stride > 1:
        stages.append(("dp", samples // stride, stride))
    return stages


def place(axis, size, stride):
    return lax.rem(lax.axis_index(axis) // stride, size)


def partner(axis, size, stride, step):
    own = place(axis, size, stride)
    other = lax.rem(own + step, size)
    dp, space = lax.axis_index("dp"), lax.axis_index("space")
    if axis == "space":
        return other, (dp, other)
    return other, (dp + (other - own) * stride, space)


def rows_at(start, count):
    return pl.ds(pl.multiple_of(start, ROW_TILE), count)


class Reduction:
    def __init__(self, stages, total, outgoing, gathered, landing, sems):
        self.stages, self.total, self.outgoing = stages, total, outgoing
        self.gathered, self.landing, self.sems = gathered, landing, sems
        self.start, self.length = 0, total.shape[0]
        self.starts, self.copies, self.sent, self.used = [], [], [], 0

    def copy(self, source, target, device):
        send, recv = self.sems
        made = pltpu.make_async_remote_copy(
            src_ref=source,
            dst_ref=target,
            send_sem=send.at[self.used],
            recv_sem=recv.at[self.used],
            device_id=device,
            device_id_type=pl.DeviceIdType.MESH,
        )
        self.used += 1
        made.start()
        self.copies.append(made)

    def scatter_start(self, index):
        axis, size, stride = self.stages[index]
        piece = self.length // size
        for step in range(1, size):
            other, device = partner(axis, size, stride, step)
            window = rows_at(self.start + other * piece, piece)
            self.outgoing[window] = self.total[window].astype(jnp.bfloat16)
            self.copy(self.outgoing.at[window], self.landing[index].at[step - 1], device)
        self.starts.append(self.start)
        self.start = self.start + place(axis, size, stride) * piece
        self.length = piece

    def scatter_finish(self, index):
        window = rows_at(self.start, self.length)
        value = self.total[window]
        for step, made in enumerate(self.copies):
            made.wait_recv()
            value = value + self.landing[index][step].astype(jnp.float32)
        self.total[window] = value
        self.sent += self.copies
        self.copies = []

    def gather_own(self):
        window = rows_at(self.start, self.length)
        self.gathered[window] = self.total[window].astype(jnp.bfloat16)

    def gather_start(self, index):
        axis, size, stride = self.stages[index]
        window = rows_at(self.start, self.length)
        for step in range(1, size):
            _, device = partner(axis, size, stride, step)
            self.copy(self.gathered.at[window], self.gathered.at[window], device)
        self.start = self.starts[index]
        self.length = self.length * size

    def gather_finish(self):
        for made in self.copies:
            made.wait_recv()
        self.sent += self.copies
        self.copies = []

    def drain(self):
        for made in self.sent:
            made.wait_send()


def reduction_rows(rows, devices):
    return -(-rows // (devices * ROW_TILE)) * ROW_TILE * devices


def reduction_scratch(stages, rows):
    shapes = [
        pltpu.VMEM((rows, LANES), jnp.float32),
        pltpu.VMEM((rows, LANES), jnp.bfloat16),
        pltpu.VMEM((rows, LANES), jnp.bfloat16),
    ]
    length, count = rows, 0
    for _, size, _ in stages:
        length //= size
        count += 2 * (size - 1)
        shapes.append(pltpu.VMEM((size - 1, length, LANES), jnp.bfloat16))
    return shapes + [pltpu.SemaphoreType.DMA((count,)), pltpu.SemaphoreType.DMA((count,))]


def greet(stages):
    barrier = pltpu.get_barrier_semaphore()
    count = 0
    for axis, size, stride in stages:
        for step in range(1, size):
            _, device = partner(axis, size, stride, step)
            pl.semaphore_signal(barrier, inc=1, device_id=device, device_id_type=pl.DeviceIdType.MESH)
            count += 1
    pl.semaphore_wait(barrier, count)


def widened(edges, center, low, high):
    first = (edges[0].astype(jnp.float32) * low).astype(jnp.bfloat16)
    last = (edges[1].astype(jnp.float32) * high).astype(jnp.bfloat16)
    return jnp.concatenate([first, center, last], axis=1)


def fill_patches(patches, planes, row_count, col_count):
    chans, total = planes.shape
    cells = row_count * col_count
    span = total - 2 * cells
    lane = lax.broadcasted_iota(jnp.int32, (1, total), 1)
    col = lane % col_count
    row = lane // col_count % row_count
    for row_tap in range(3):
        for col_tap in range(3):
            row_at, col_at = row + (row_tap - 1), col + (col_tap - 1)
            inside = (row_at >= 0) & (row_at < row_count) & (col_at >= 0) & (col_at < col_count)
            offset = (row_tap - 1) * col_count + col_tap - 1
            moved = planes
            if offset:
                moved = pltpu.roll(planes, -offset % total, 1)
                moved = moved * jnp.where(inside, 1.0, 0.0).astype(jnp.bfloat16)
            for depth_tap in range(3):
                tap = (depth_tap * 3 + row_tap) * 3 + col_tap
                patches[tap * chans : (tap + 1) * chans] = moved[
                    :, depth_tap * cells : depth_tap * cells + span
                ]


def gelu_parts(values):
    scale = 0.7978845608028654
    square = values * values
    bend = jnp.tanh(scale * values * (1.0 + 0.044715 * square))
    half = 0.5 * (1.0 + bend)
    slope = half + 0.5 * values * (1.0 - bend * bend) * (scale * (1.0 + 0.134145 * square))
    return values * half, slope


def contract(left, right, left_dim, right_dim):
    return lax.dot_general(
        left, right, (((left_dim,), (right_dim,)), ((), ())), preferred_element_type=jnp.float32
    )


def pool_cells(values, row_count, col_count):
    cells = row_count * col_count
    pairs = [
        values[:, 2 * d * cells : (2 * d + 1) * cells] + values[:, (2 * d + 1) * cells : (2 * d + 2) * cells]
        for d in range(values.shape[1] // (2 * cells))
    ]
    paired = jnp.concatenate(pairs, axis=1)
    span = paired.shape[1]
    paired = paired + pltpu.roll(paired, span - 1, 1)
    paired = paired + pltpu.roll(paired, span - col_count, 1)
    small = cells // 4
    target = lax.broadcasted_iota(jnp.int32, (span, span // 4), 1)
    cell = target % small
    corner = (
        target // small * cells
        + cell // (col_count // 2) * (2 * col_count)
        + cell % (col_count // 2) * 2
    )
    here = lax.broadcasted_iota(jnp.int32, (span, span // 4), 0)
    picks = jnp.where(here == corner, 1.0, 0.0).astype(jnp.bfloat16)
    return contract((paired * 0.125).astype(jnp.bfloat16), picks, 1, 0).astype(jnp.bfloat16)


def spread_cells(values, row_count, col_count):
    cells = row_count * col_count
    chans, small_span = values.shape
    span = small_span * 8
    cell = lax.broadcasted_iota(jnp.int32, (small_span, span), 1)
    source = (
        cell // (2 * cells) * (cells // 4)
        + cell % cells // (2 * col_count) * (col_count // 2)
        + cell % col_count // 2
    )
    here = lax.broadcasted_iota(jnp.int32, (small_span, span), 0)
    copies = jnp.where(here == source, 1.0, 0.0).astype(jnp.bfloat16)
    high = values.astype(jnp.bfloat16)
    rest = values - high.astype(jnp.float32)
    middle = rest.astype(jnp.bfloat16)
    low = (rest - middle.astype(jnp.float32)).astype(jnp.bfloat16)
    wide = contract(jnp.concatenate([high, middle, low], axis=0), copies, 1, 0)
    return wide[:chans] + wide[chans : 2 * chans] + wide[2 * chans :]


def block_kernel(plans, layout, scale, *refs):
    refs = list(refs)

    def take(count):
        taken = refs[:count]
        del refs[:count]
        return taken

    source_ref, cot_ref, mid_ref, deep_ref = take(4)
    grad_in_ref, mid_out, deep_out = take(3)
    mid_patches, deep_patches, deep_back, mid_back, mid_flip, deep_flip = take(6)
    edges = [take(2) for _ in range(4)]
    edge_send, edge_recv = take(2)
    works = []
    for stages in plans:
        total, outgoing, gathered = take(3)
        landing = take(len(stages))
        works.append(Reduction(stages, total, outgoing, gathered, landing, take(2)))
    first, second, third = works
    row_count, col_count = layout
    cells = row_count * col_count
    small = cells // 4
    chans1 = source_ref.shape[0]
    chans2, chans3 = deep_ref.shape[0] // 27, deep_ref.shape[1]
    dp, space = lax.axis_index("dp"), lax.axis_index("space")
    slabs = lax.axis_size("space")
    low = jnp.where(space > 0, 1.0, 0.0)
    high = jnp.where(space < slabs - 1, 1.0, 0.0)

    def swap_start(index, planes, cells_here):
        leaving, arriving = edges[index]
        leaving[0] = planes[:, :cells_here]
        leaving[1] = planes[:, planes.shape[1] - cells_here :]
        made = []
        for side, other in ((0, lax.rem(space + slabs - 1, slabs)), (1, lax.rem(space + 1, slabs))):
            made.append(
                pltpu.make_async_remote_copy(
                    src_ref=leaving.at[side],
                    dst_ref=arriving.at[1 - side],
                    send_sem=edge_send.at[2 * index + side],
                    recv_sem=edge_recv.at[2 * index + side],
                    device_id=(dp, other),
                    device_id_type=pl.DeviceIdType.MESH,
                )
            )
            made[-1].start()
        return made

    def swap_finish(index, made, planes):
        for one in made:
            one.wait_recv()
        return widened(edges[index][1], planes, low, high)

    greet(plans[0])
    source = source_ref[...]
    swap0 = swap_start(0, source, cells)
    for tap in range(27):
        mid_flip[:, tap * chans2 : (tap + 1) * chans2] = mid_ref[(26 - tap) * chans1 : (27 - tap) * chans1]
        deep_flip[:, tap * chans3 : (tap + 1) * chans3] = deep_ref[(26 - tap) * chans2 : (27 - tap) * chans2]
    deep_rows = deep_ref.shape[0]
    cut = deep_rows // 2
    half = mid_out.shape[0] // 2
    for work, used in ((first, cut), (second, deep_rows - cut), (third, half)):
        spare = work.total.shape[0] - used
        if spare:
            work.total[used:] = jnp.zeros((spare, LANES), jnp.float32)
    fill_patches(mid_patches, swap_finish(0, swap0, source), row_count, col_count)
    mid_pre = contract(mid_ref[...], mid_patches[...], 0, 0)
    activated, mid_slope = gelu_parts(mid_pre)
    pooled = pool_cells(activated, row_count, col_count)
    swap1 = swap_start(1, pooled, small)
    fill_patches(deep_patches, swap_finish(1, swap1, pooled), row_count // 2, col_count // 2)
    deep_pre = contract(deep_ref[...], deep_patches[...], 0, 0)
    deep_grad = (cot_ref[...].astype(jnp.float32) * gelu_parts(deep_pre)[1]).astype(jnp.bfloat16)
    swap2 = swap_start(2, deep_grad, small)
    first.total[:cut] = contract(deep_patches[:cut], deep_grad, 1, 1)
    first.scatter_start(0)
    second.total[: deep_rows - cut] = contract(deep_patches[cut:], deep_grad, 1, 1)
    second.scatter_start(0)
    fill_patches(deep_back, swap_finish(2, swap2, deep_grad), row_count // 2, col_count // 2)
    back = contract(deep_flip[...], deep_back[...], 1, 0)
    upstream = spread_cells(back, row_count, col_count) * 0.125
    mid_grad = (upstream * mid_slope).astype(jnp.bfloat16)
    swap3 = swap_start(3, mid_grad, cells)
    depth = len(plans[0])

    def advance(work, index):
        work.scatter_finish(index)
        if index + 1 < depth:
            work.scatter_start(index + 1)
        else:
            work.gather_own()
            work.gather_start(depth - 1)

    def collect(work, index):
        work.gather_finish()
        if index:
            work.gather_start(index - 1)

    advance(first, 0)
    advance(second, 0)
    third.total[:half] = jnp.concatenate(
        [contract(mid_patches[:half], mid_grad, 1, 1), contract(mid_patches[half:], mid_grad, 1, 1)], axis=1
    )
    third.scatter_start(0)
    advance(first, 1)
    advance(second, 1)
    fill_patches(mid_back, swap_finish(3, swap3, mid_grad), row_count, col_count)
    advance(third, 0)
    grad_in_ref[...] = contract(mid_flip[...], mid_back[...], 1, 0).astype(jnp.bfloat16)
    for index in range(2, depth):
        advance(first, index)
        advance(second, index)
        advance(third, index - 1)
    collect(first, depth - 1)
    collect(second, depth - 1)
    advance(third, depth - 1)
    for index in reversed(range(depth - 1)):
        collect(first, index)
        collect(second, index)
        collect(third, index + 1)
    deep_out[:cut] = first.gathered[:cut].astype(jnp.float32) * scale
    deep_out[cut:] = second.gathered[: deep_rows - cut].astype(jnp.float32) * scale
    collect(third, 0)
    packed = third.gathered[:half].astype(jnp.float32) * scale
    mid_out[:half] = packed[:, : mid_out.shape[1]]
    mid_out[half:] = packed[:, mid_out.shape[1] :]
    for one in swap0 + swap1 + swap2 + swap3:
        one.wait_send()
    for work in works:
        work.drain()


def shards(activations, cotangent, weight_mid, weight_deep):
    samples, slabs = lax.axis_size("dp"), lax.axis_size("space")
    stages = group_stages(samples, slabs)
    swapped = [stages[0], stages[2], stages[1]] + stages[3:]
    plans = (stages, swapped, stages)
    chans1, chans2, chans3 = weight_mid.shape[3], weight_mid.shape[4], weight_deep.shape[4]
    source = activations[0].reshape(chans1, -1)
    upstream = cotangent[0].reshape(chans3, -1)
    mid_flat = weight_mid.reshape(-1, chans2)
    deep_flat = weight_deep.reshape(-1, chans3)
    cells, small = source.shape[1], upstream.shape[1]
    plane, small_plane = ROWS * COLS, ROWS * COLS // 4
    half_rows = reduction_rows(-(-deep_flat.shape[0] // 2), samples * slabs)
    mid_rows = reduction_rows(mid_flat.shape[0] // 2, samples * slabs)
    scratch = [
        pltpu.VMEM((27 * chans1, cells), jnp.bfloat16),
        pltpu.VMEM((27 * chans2, small), jnp.bfloat16),
        pltpu.VMEM((27 * chans3, small), jnp.bfloat16),
        pltpu.VMEM((27 * chans2, cells), jnp.bfloat16),
        pltpu.VMEM((chans1, 27 * chans2), jnp.bfloat16),
        pltpu.VMEM((chans2, 27 * chans3), jnp.bfloat16),
    ]
    for chans, width in ((chans1, plane), (chans2, small_plane), (chans3, small_plane), (chans2, plane)):
        scratch += [pltpu.VMEM((2, chans, width), jnp.bfloat16)] * 2
    scratch += [pltpu.SemaphoreType.DMA((8,)), pltpu.SemaphoreType.DMA((8,))]
    for plan, rows in zip(plans, (half_rows, half_rows, mid_rows)):
        scratch += reduction_scratch(plan, rows)
    grad_in, mid_sum, deep_sum = pl.pallas_call(
        functools.partial(block_kernel, plans, (ROWS, COLS), 1.0 / samples),
        out_shape=[
            jax.ShapeDtypeStruct(source.shape, jnp.bfloat16),
            jax.ShapeDtypeStruct(mid_flat.shape, jnp.float32),
            jax.ShapeDtypeStruct(deep_flat.shape, jnp.float32),
        ],
        in_specs=[pl.BlockSpec(memory_space=pltpu.VMEM)] * 4,
        out_specs=[pl.BlockSpec(memory_space=pltpu.VMEM)] * 3,
        scratch_shapes=scratch,
        compiler_params=pltpu.CompilerParams(
            collective_id=0, has_side_effects=True, vmem_limit_bytes=56 * 1024 * 1024
        ),
    )(source, upstream, mid_flat, deep_flat)
    return (
        grad_in.reshape(activations.shape),
        mid_sum.reshape(weight_mid.shape),
        deep_sum.reshape(weight_deep.shape),
    )


def solution(mesh):
    in_specs = (P("dp", None, "space", None), P("dp", None, "space", None), P(), P())
    out_specs = (P("dp", None, "space", None), P(), P())
    return jax.shard_map(shards, mesh=mesh, in_specs=in_specs, out_specs=out_specs, check_vma=False)
```

time: 109 us -> 46.2 us (0.42)
  local copies, waits for them, and re-layouts: 35.8 us -> 6.45 us
  starting transfers between devices: 13 us -> 0 us
  other arithmetic: 12.8 us -> 0 us
  matrix products: 10.8 us -> 0 us
  Pallas kernels: 33.6 us -> 38.8 us
  between operations: 2.12 us -> 0.66 us
    unnamed x103 -> x7, local copies, waits for them, and re-layouts: 20.1 us -> 3.36 us
    ppermute x6 -> x0, starting transfers between devices: 13 us -> none  [the longest x3 8.76 us: extended(): lax.ppermute(lax.slice_in_dim(block, 0, width, axis=dim), axis, backward)]
    another operation x50 -> x0, other arithmetic: 12.1 us -> none  [tap_patches(): jnp.stack([shifted(planes, row_tap - 1, col_tap - 1, row_count, col_count...]
    dot_general x56 -> x0, matrix products: 10.8 us -> none  [the longest x36 7.35 us: conv_cube(): lax.dot_general(tap_block, patches, (((0,), (0,)), ((), ())), preferred_e...]
    slice x25 -> x0, local copies, waits for them, and re-layouts: 6.75 us -> none  [the longest x22 5.03 us: conv_cube(): tap_block = kernel[depth_tap, row_tap].reshape(3 * chans_in, chans_out)]
    pallas_call x1, Pallas kernels: 33.6 us -> 38.8 us  [shards(): pl.pallas_call(functools.partial(block_kernel, plans, (ROWS, COLS), 1.0 /...]
    another operation x28 -> x1, local copies, waits for them, and re-layouts: 6.34 us -> 1.51 us  [shards(): upstream = cotangent[0].reshape(chans3, -1)]
  transfers between devices with their start and end apart: 6 -> 0, of which waited for: 0 -> 0; matrix products, arithmetic and copies ran while one was open for 17% -> 0% of each run, Pallas kernels for 31% -> 0%
where the time goes in v2:
time: 46.2 us; the launch traced here: 45.9 us
  Pallas kernels  38.8 us (84%)
  local copies, waits for them, and re-layouts  6.45 us (14%)
  between operations  0.66 us (1%)
    pallas_call x1, Pallas kernels, shards(): pl.pallas_call(functools.partial(block_kernel, plans, (ROWS, COLS), 1.0 /...  38.8 us
    unnamed x7, local copies, waits for them, and re-layouts  3.36 us
    reshape x1, local copies, waits for them, and re-layouts, shards(): grad_in.reshape(activations.shape)  1.58 us
    another operation x1, local copies, waits for them, and re-layouts, shards(): upstream = cotangent[0].reshape(chans3, -1)  1.51 us

profile of v2, /device:TPU:1, one launch (start us, length us, event | category | flops | bytes accessed | tf_op | source)
XLA Modules:
  0.0 45.9 jit_solution(5744474289677168905)
XLA Ops:
  0.6 0.0 copy-start.1
  0.6 1.5 %copy.8.refs_1_ = bf16[128,128]{1,0:T(8,128)(2,1)} copy(bf16[128,128]{0,1:T(8,128)(2,1)} %bitcast.14) | data formatting | bytes 65536 | tf_op jit(solution)/shard_map/reshape;squeeze | solution.py:368
  2.1 0.0 copy-done.1
  2.1 0.6 %copy.9 = bf16[4,8,4,256]{3,1,2,0:T(8,128)(2,1)} copy(bf16[4,8,4,256]{3,2,1,0:T(4,128)(2,1)S(1)} %bitcast.13) | data formatting | bytes 131072
  2.8 38.8 %shard_map.67 = (bf16[32,1024]{1,0:T(8,128)(2,1)}, f32[864,64]{1,0:T(8,128)}, f32[1728,128]{1,0:T(8,128)}) custom-call(bf16[32,1024]{1,0:T(8,128)(2,1)} %bitcast.11, bf16[128,128]{1,0:T(8,128)(2,1)} %copy.8.refs_1_, bf16[864,64]{1,0:T(8,128)(2,1)} %bitcast.12, bf16[1728,128]{1,0:T(8,128)(2,1)} %bitcast.10), custom_call_target="tpu_custom_call" | custom-call | tf_op jit(solution)/shard_map/pallas_call | solution.py:388
  41.6 0.0 copy-start
  41.6 1.6 %reshape.23 = bf16[1,32,4,256]{3,2,1,0:T(4,128)(2,1)} reshape(bf16[32,1024]{1,0:T(8,128)(2,1)} %get-tuple-element.6) | data formatting | bytes 131072 | tf_op jit(solution)/shard_map/reshape | solution.py:403
  43.2 1.8 %copy.12 = f32[3,3,3,32,64]{4,3,2,1,0:T(8,128)} copy(f32[3,3,3,32,64]{4,3,2,1,0:T(8,128)} %bitcast.9) | data formatting | bytes 442368
  45.0 0.0 copy-done
  45.0 0.9 %copy.13 = f32[3,3,3,64,128]{4,3,2,1,0:T(8,128)} copy(f32[3,3,3,64,128]{4,3,2,1,0:T(8,128)S(1)} %bitcast.8) | data formatting | bytes 1769472
Async XLA Ops:
  0.6 1.5 %copy-start.1 = (bf16[1,32,4,256]{3,2,1,0:T(4,128)(2,1)S(1)}, bf16[1,32,4,256]{3,2,1,0:T(4,128)(2,1)}, u32[]{:S(2)}) copy-start(bf16[1,32,4,256]{3,2,1,0:T(4,128)(2,1)} %param.4) | copy-start | bytes 196612
  41.6 3.4 %copy-start = (f32[1728,128]{1,0:T(8,128)S(1)}, f32[1728,128]{1,0:T(8,128)}, u32[]{:S(2)}) copy-start(f32[1728,128]{1,0:T(8,128)} %get-tuple-element.8) | copy-start | bytes 2654212

commit v3 on v2

--- a/solution.py
+++ b/solution.py
@@ -16,7 +16,7 @@
 def group_stages(samples, slabs):
     stages = [("space", slabs, 1)]
     stride = 1
-    for size in (2, 2, 4):
+    for size in (4, 4):
         if samples // stride % size == 0:
             stages.append(("dp", size, stride))
             stride *= size
@@ -138,42 +138,57 @@
     pl.semaphore_wait(barrier, count)
 
 
-def widened(edges, center, low, high):
+def moved_planes(planes, row_tap, col_tap, row_count, col_count):
+    offset = (row_tap - 1) * col_count + col_tap - 1
+    if not offset:
+        return planes
+    total = planes.shape[1]
+    lane = lax.broadcasted_iota(jnp.int32, (1, total), 1)
+    col_at = lane % col_count + (col_tap - 1)
+    row_at = lane // col_count % row_count + (row_tap - 1)
+    inside = (row_at >= 0) & (row_at < row_count) & (col_at >= 0) & (col_at < col_count)
+    keep = jnp.where(inside, 1.0, 0.0).astype(jnp.bfloat16)
+    return pltpu.roll(planes, -offset % total, 1) * keep
+
+
+def plane_taps():
+    return [(row_tap, col_tap) for row_tap in range(3) for col_tap in range(3)]
+
+
+def tap_rows(depth_tap, row_tap, col_tap, chans):
+    tap = (depth_tap * 3 + row_tap) * 3 + col_tap
+    return slice(tap * chans, (tap + 1) * chans)
+
+
+def fill_inner(patches, planes, row_count, col_count):
+    chans, span = planes.shape
+    cells = row_count * col_count
+    for taps in plane_taps():
+        moved = moved_planes(planes, *taps, row_count, col_count)
+        patches[tap_rows(0, *taps, chans), cells:] = moved[:, : span - cells]
+        patches[tap_rows(1, *taps, chans)] = moved
+        patches[tap_rows(2, *taps, chans), : span - cells] = moved[:, cells:]
+
+
+def fill_outer(patches, edges, low, high, row_count, col_count):
+    chans, cells = edges.shape[1:]
+    span = patches.shape[1]
     first = (edges[0].astype(jnp.float32) * low).astype(jnp.bfloat16)
     last = (edges[1].astype(jnp.float32) * high).astype(jnp.bfloat16)
-    return jnp.concatenate([first, center, last], axis=1)
-
-
-def fill_patches(patches, planes, row_count, col_count):
-    chans, total = planes.shape
-    cells = row_count * col_count
-    span = total - 2 * cells
-    lane = lax.broadcasted_iota(jnp.int32, (1, total), 1)
-    col = lane % col_count
-    row = lane // col_count % row_count
-    for row_tap in range(3):
-        for col_tap in range(3):
-            row_at, col_at = row + (row_tap - 1), col + (col_tap - 1)
-            inside = (row_at >= 0) & (row_at < row_count) & (col_at >= 0) & (col_at < col_count)
-            offset = (row_tap - 1) * col_count + col_tap - 1
-            moved = planes
-            if offset:
-                moved = pltpu.roll(planes, -offset % total, 1)
-                moved = moved * jnp.where(inside, 1.0, 0.0).astype(jnp.bfloat16)
-            for depth_tap in range(3):
-                tap = (depth_tap * 3 + row_tap) * 3 + col_tap
-                patches[tap * chans : (tap + 1) * chans] = moved[
-                    :, depth_tap * cells : depth_tap * cells + span
-                ]
-
-
-def gelu_parts(values):
-    scale = 0.7978845608028654
-    square = values * values
-    bend = jnp.tanh(scale * values * (1.0 + 0.044715 * square))
-    half = 0.5 * (1.0 + bend)
-    slope = half + 0.5 * values * (1.0 - bend * bend) * (scale * (1.0 + 0.134145 * square))
-    return values * half, slope
+    planes = jnp.concatenate([first, last], axis=1)
+    for taps in plane_taps():
+        moved = moved_planes(planes, *taps, row_count, col_count)
+        patches[tap_rows(0, *taps, chans), :cells] = moved[:, :cells]
+        patches[tap_rows(2, *taps, chans), span - cells :] = moved[:, cells:]
+
+
+def gelu_bend(values):
+    return jnp.tanh(0.7978845608028654 * values * (1.0 + 0.044715 * values * values))
+
+
+def gelu_slope(values, bend):
+    outer = 0.7978845608028654 * (1.0 + 0.134145 * values * values)
+    return 0.5 * (1.0 + bend) + 0.5 * values * (1.0 - bend * bend) * outer
 
 
 def contract(left, right, left_dim, right_dim):
@@ -225,7 +240,25 @@
     return wide[:chans] + wide[chans : 2 * chans] + wide[2 * chans :]
 
 
-def block_kernel(plans, layout, scale, *refs):
+def merged_planes(planes):
+    wide = planes.astype(jnp.float32)
+    parts = [wide[:, d, :] for d in range(planes.shape[1])]
+    return jnp.concatenate(parts, axis=1).astype(planes.dtype)
+
+
+def finish_kernel(scale, grad_in_ref, mid_ref, deep_ref, grad_in_out, mid_out, deep_out):
+    half = mid_ref.shape[0]
+    cells = grad_in_out.shape[2]
+    packed = mid_ref[...].astype(jnp.float32) * scale
+    mid_out[:half] = packed[:, : mid_out.shape[1]]
+    mid_out[half:] = packed[:, mid_out.shape[1] :]
+    deep_out[...] = deep_ref[...].astype(jnp.float32) * scale
+    grad_in = grad_in_ref[...]
+    planes = [grad_in[:, d * cells : (d + 1) * cells] for d in range(grad_in_out.shape[1])]
+    grad_in_out[...] = jnp.stack(planes, axis=1).astype(jnp.bfloat16)
+
+
+def block_kernel(plans, layout, *refs):
     refs = list(refs)
 
     def take(count):
@@ -273,41 +306,45 @@
             made[-1].start()
         return made
 
-    def swap_finish(index, made, planes):
+    def swap_finish(index, made, patches, row_count, col_count):
         for one in made:
             one.wait_recv()
-        return widened(edges[index][1], planes, low, high)
+        fill_outer(patches, edges[index][1], low, high, row_count, col_count)
 
     greet(plans[0])
-    source = source_ref[...]
+    source = merged_planes(source_ref[...])
     swap0 = swap_start(0, source, cells)
     for tap in range(27):
         mid_flip[:, tap * chans2 : (tap + 1) * chans2] = mid_ref[(26 - tap) * chans1 : (27 - tap) * chans1]
         deep_flip[:, tap * chans3 : (tap + 1) * chans3] = deep_ref[(26 - tap) * chans2 : (27 - tap) * chans2]
     deep_rows = deep_ref.shape[0]
     cut = deep_rows // 2
-    half = mid_out.shape[0] // 2
+    half = mid_out.shape[0]
     for work, used in ((first, cut), (second, deep_rows - cut), (third, half)):
         spare = work.total.shape[0] - used
         if spare:
             work.total[used:] = jnp.zeros((spare, LANES), jnp.float32)
-    fill_patches(mid_patches, swap_finish(0, swap0, source), row_count, col_count)
+    fill_inner(mid_patches, source, row_count, col_count)
+    swap_finish(0, swap0, mid_patches, row_count, col_count)
     mid_pre = contract(mid_ref[...], mid_patches[...], 0, 0)
-    activated, mid_slope = gelu_parts(mid_pre)
-    pooled = pool_cells(activated, row_count, col_count)
+    mid_bend = gelu_bend(mid_pre)
+    pooled = pool_cells(0.5 * mid_pre * (1.0 + mid_bend), row_count, col_count)
     swap1 = swap_start(1, pooled, small)
-    fill_patches(deep_patches, swap_finish(1, swap1, pooled), row_count // 2, col_count // 2)
+    fill_inner(deep_patches, pooled, row_count // 2, col_count // 2)
+    upstream = cot_ref[...].astype(jnp.float32).T
+    mid_slope = gelu_slope(mid_pre, mid_bend)
+    swap_finish(1, swap1, deep_patches, row_count // 2, col_count // 2)
     deep_pre = contract(deep_ref[...], deep_patches[...], 0, 0)
-    deep_grad = (cot_ref[...].astype(jnp.float32) * gelu_parts(deep_pre)[1]).astype(jnp.bfloat16)
+    deep_grad = (upstream * gelu_slope(deep_pre, gelu_bend(deep_pre))).astype(jnp.bfloat16)
     swap2 = swap_start(2, deep_grad, small)
     first.total[:cut] = contract(deep_patches[:cut], deep_grad, 1, 1)
     first.scatter_start(0)
     second.total[: deep_rows - cut] = contract(deep_patches[cut:], deep_grad, 1, 1)
     second.scatter_start(0)
-    fill_patches(deep_back, swap_finish(2, swap2, deep_grad), row_count // 2, col_count // 2)
+    fill_inner(deep_back, deep_grad, row_count // 2, col_count // 2)
+    swap_finish(2, swap2, deep_back, row_count // 2, col_count // 2)
     back = contract(deep_flip[...], deep_back[...], 1, 0)
-    upstream = spread_cells(back, row_count, col_count) * 0.125
-    mid_grad = (upstream * mid_slope).astype(jnp.bfloat16)
+    mid_grad = (spread_cells(back, row_count, col_count) * 0.125 * mid_slope).astype(jnp.bfloat16)
     swap3 = swap_start(3, mid_grad, cells)
     depth = len(plans[0])
 
@@ -332,9 +369,10 @@
     third.scatter_start(0)
     advance(first, 1)
     advance(second, 1)
-    fill_patches(mid_back, swap_finish(3, swap3, mid_grad), row_count, col_count)
+    fill_inner(mid_back, mid_grad, row_count, col_count)
+    swap_finish(3, swap3, mid_back, row_count, col_count)
     advance(third, 0)
-    grad_in_ref[...] = contract(mid_flip[...], mid_back[...], 1, 0).astype(jnp.bfloat16)
+    grad_in_ref[...] = contract(mid_flip[...], mid_back[...], 1, 0)
     for index in range(2, depth):
         advance(first, index)
         advance(second, index)
@@ -346,12 +384,10 @@
         collect(first, index)
         collect(second, index)
         collect(third, index + 1)
-    deep_out[:cut] = first.gathered[:cut].astype(jnp.float32) * scale
-    deep_out[cut:] = second.gathered[: deep_rows - cut].astype(jnp.float32) * scale
+    deep_out[:cut] = first.gathered[:cut]
+    deep_out[cut:] = second.gathered[: deep_rows - cut]
     collect(third, 0)
-    packed = third.gathered[:half].astype(jnp.float32) * scale
-    mid_out[:half] = packed[:, : mid_out.shape[1]]
-    mid_out[half:] = packed[:, mid_out.shape[1] :]
+    mid_out[...] = third.gathered[:half]
     for one in swap0 + swap1 + swap2 + swap3:
         one.wait_send()
     for work in works:
@@ -361,14 +397,13 @@
 def shards(activations, cotangent, weight_mid, weight_deep):
     samples, slabs = lax.axis_size("dp"), lax.axis_size("space")
     stages = group_stages(samples, slabs)
-    swapped = [stages[0], stages[2], stages[1]] + stages[3:]
-    plans = (stages, swapped, stages)
+    plans = (stages, stages, stages)
     chans1, chans2, chans3 = weight_mid.shape[3], weight_mid.shape[4], weight_deep.shape[4]
-    source = activations[0].reshape(chans1, -1)
-    upstream = cotangent[0].reshape(chans3, -1)
+    source = activations[0]
+    upstream = jnp.transpose(cotangent[0], (1, 2, 0)).reshape(-1, chans3)
     mid_flat = weight_mid.reshape(-1, chans2)
     deep_flat = weight_deep.reshape(-1, chans3)
-    cells, small = source.shape[1], upstream.shape[1]
+    cells, small = source.shape[1] * source.shape[2], upstream.shape[0]
     plane, small_plane = ROWS * COLS, ROWS * COLS // 4
     half_rows = reduction_rows(-(-deep_flat.shape[0] // 2), samples * slabs)
     mid_rows = reduction_rows(mid_flat.shape[0] // 2, samples * slabs)
@@ -385,20 +420,32 @@
     scratch += [pltpu.SemaphoreType.DMA((8,)), pltpu.SemaphoreType.DMA((8,))]
     for plan, rows in zip(plans, (half_rows, half_rows, mid_rows)):
         scratch += reduction_scratch(plan, rows)
+    room = 24 * 1024 * 1024 + 12 * LANES * (2 * half_rows + mid_rows)
     grad_in, mid_sum, deep_sum = pl.pallas_call(
-        functools.partial(block_kernel, plans, (ROWS, COLS), 1.0 / samples),
+        functools.partial(block_kernel, plans, (ROWS, COLS)),
+        out_shape=[
+            jax.ShapeDtypeStruct((chans1, cells), jnp.float32),
+            jax.ShapeDtypeStruct((mid_flat.shape[0] // 2, LANES), jnp.bfloat16),
+            jax.ShapeDtypeStruct(deep_flat.shape, jnp.bfloat16),
+        ],
+        in_specs=[pl.BlockSpec(memory_space=pltpu.VMEM)] * 4,
+        out_specs=[pl.BlockSpec(memory_space=pltpu.VMEM)] * 3,
+        scratch_shapes=scratch,
+        compiler_params=pltpu.CompilerParams(
+            collective_id=0, has_side_effects=True, vmem_limit_bytes=min(room, 56 * 1024 * 1024)
+        ),
+    )(source, upstream, mid_flat, deep_flat)
+    grad_in, mid_sum, deep_sum = pl.pallas_call(
+        functools.partial(finish_kernel, 1.0 / samples),
         out_shape=[
             jax.ShapeDtypeStruct(source.shape, jnp.bfloat16),
             jax.ShapeDtypeStruct(mid_flat.shape, jnp.float32),
             jax.ShapeDtypeStruct(deep_flat.shape, jnp.float32),
         ],
-        in_specs=[pl.BlockSpec(memory_space=pltpu.VMEM)] * 4,
+        in_specs=[pl.BlockSpec(memory_space=pltpu.VMEM)] * 3,
         out_specs=[pl.BlockSpec(memory_space=pltpu.VMEM)] * 3,
-        scratch_shapes=scratch,
-        compiler_params=pltpu.CompilerParams(
-            collective_id=0, has_side_effects=True, vmem_limit_bytes=56 * 1024 * 1024
-        ),
-    )(source, upstream, mid_flat, deep_flat)
+        compiler_params=pltpu.CompilerParams(vmem_limit_bytes=16 * 1024 * 1024),
+    )(grad_in, mid_sum, deep_sum)
     return (
         grad_in.reshape(activations.shape),
         mid_sum.reshape(weight_mid.shape),

time: 46.2 us -> 38.3 us (0.83)
  Pallas kernels: 38.8 us -> 33.8 us
  local copies, waits for them, and re-layouts: 6.45 us -> 3.54 us
    pallas_call x1 -> x2, Pallas kernels: 38.8 us -> 33.8 us  [the longest x1 32.6 us: shards(): pl.pallas_call(functools.partial(block_kernel, plans, (ROWS, COLS)), out_...]
    reshape x1 -> x0, local copies, waits for them, and re-layouts: 1.58 us -> none  [shards(): grad_in.reshape(activations.shape)]
    another operation x1 -> x0, local copies, waits for them, and re-layouts: 1.51 us -> none  [shards(): upstream = cotangent[0].reshape(chans3, -1)]
    unnamed x7 -> x8, local copies, waits for them, and re-layouts: 3.36 us -> 3.54 us
where the time goes in v3:
time: 38.3 us; the launch traced here: 38 us
  Pallas kernels  33.8 us (88%)
  local copies, waits for them, and re-layouts  3.54 us (9%)
  between operations  0.65 us (2%)
    pallas_call x1, Pallas kernels, shards(): pl.pallas_call(functools.partial(block_kernel, plans, (ROWS, COLS)), out_...  32.6 us
    unnamed x8, local copies, waits for them, and re-layouts  3.54 us
    pallas_call x1, Pallas kernels, shards(): pl.pallas_call(functools.partial(finish_kernel, 1.0 / samples), out_shape...  1.21 us

profile of v3, /device:TPU:1, one launch (start us, length us, event | category | flops | bytes accessed | tf_op | source)
XLA Modules:
  0.0 38.0 jit_solution(2383223641643849888)
XLA Ops:
  0.6 0.0 copy-start
  0.6 1.0 %copy-done = bf16[3,3,3,64,128]{4,3,2,1,0:T(8,128)(2,1)S(1)} copy-done((bf16[3,3,3,64,128]{4,3,2,1,0:T(8,128)(2,1)S(1)}, bf16[3,3,3,64,128]{4,3,2,1,0:T(8,128)(2,1)}, u32[]{:S(2)}) %copy-start) | copy-done | bytes 442392
  1.6 0.0 copy-start.1
  1.6 0.9 %copy-done.1 = bf16[3,3,3,32,64]{4,3,2,1,0:T(8,128)(2,1)S(1)} copy-done((bf16[3,3,3,32,64]{4,3,2,1,0:T(8,128)(2,1)S(1)}, bf16[3,3,3,32,64]{4,3,2,1,0:T(8,128)(2,1)}, u32[]{:S(2)}) %copy-start.1) | copy-done | bytes 110616
  2.6 0.0 copy-start.2
  2.6 0.8 %copy-done.2 = bf16[1,32,4,256]{3,2,1,0:T(4,128)(2,1)S(1)} copy-done((bf16[1,32,4,256]{3,2,1,0:T(4,128)(2,1)S(1)}, bf16[1,32,4,256]{3,2,1,0:T(4,128)(2,1)}, u32[]{:S(2)}) %copy-start.2) | copy-done | bytes 65560
  3.4 0.0 copy-start.3
  3.4 0.8 %copy-done.3 = bf16[1,128,2,64]{1,3,2,0:T(8,128)(2,1)S(1)} copy-done((bf16[1,128,2,64]{1,3,2,0:T(8,128)(2,1)S(1)}, bf16[1,128,2,64]{1,3,2,0:T(8,128)(2,1)}, u32[]{:S(2)}) %copy-start.3) | copy-done | bytes 32792
  4.2 32.6 %shard_map.67 = (f32[32,1024]{1,0:T(8,128)S(1)}, bf16[432,128]{1,0:T(8,128)(2,1)S(1)}, bf16[1728,128]{1,0:T(8,128)(2,1)S(1)}) custom-call(bf16[32,4,256]{2,1,0:T(4,128)(2,1)S(1)} %bitcast.13, bf16[128,128]{1,0:T(8,128)(2,1)S(1)} %bitcast.14, bf16[864,64]{1,0:T(8,128)(2,1)S(1)} %bitcast.12, bf16[1728,128]{1,0:T(8,128)(2,1)S(1)} %bitcast.11), custom_call_target="tpu_custom_call" | custom-call | tf_op jit(solution)/shard_map/pallas_call | solution.py:424
  36.8 1.2 %shard_map.68 = (bf16[32,4,256]{2,1,0:T(4,128)(2,1)}, f32[864,64]{1,0:T(8,128)}, f32[1728,128]{1,0:T(8,128)}) custom-call(f32[32,1024]{1,0:T(8,128)S(1)} %get-tuple-element.9.grad_in_ref, bf16[432,128]{1,0:T(8,128)(2,1)S(1)} %get-tuple-element.10.mid_ref, bf16[1728,128]{1,0:T(8,128)(2,1)S(1)} %get-tuple-element.11.deep_ref), custom_call_target="tpu_custom_call" | custom-call | tf_op jit(solution)/shard_map/pallas_call | solution.py:438
Async XLA Ops:
  0.6 1.0 %copy-start = (bf16[3,3,3,64,128]{4,3,2,1,0:T(8,128)(2,1)S(1)}, bf16[3,3,3,64,128]{4,3,2,1,0:T(8,128)(2,1)}, u32[]{:S(2)}) copy-start(bf16[3,3,3,64,128]{4,3,2,1,0:T(8,128)(2,1)} %param.7) | copy-start | bytes 1327108
  1.6 0.9 %copy-start.1 = (bf16[3,3,3,32,64]{4,3,2,1,0:T(8,128)(2,1)S(1)}, bf16[3,3,3,32,64]{4,3,2,1,0:T(8,128)(2,1)}, u32[]{:S(2)}) copy-start(bf16[3,3,3,32,64]{4,3,2,1,0:T(8,128)(2,1)} %param.6) | copy-start | bytes 331780
  2.6 0.8 %copy-start.2 = (bf16[1,32,4,256]{3,2,1,0:T(4,128)(2,1)S(1)}, bf16[1,32,4,256]{3,2,1,0:T(4,128)(2,1)}, u32[]{:S(2)}) copy-start(bf16[1,32,4,256]{3,2,1,0:T(4,128)(2,1)} %param.4) | copy-start | bytes 196612
  3.4 0.8 %copy-start.3 = (bf16[1,128,2,64]{1,3,2,0:T(8,128)(2,1)S(1)}, bf16[1,128,2,64]{1,3,2,0:T(8,128)(2,1)}, u32[]{:S(2)}) copy-start(bf16[1,128,2,64]{1,3,2,0:T(8,128)(2,1)} %param.5) | copy-start | bytes 98308

commit v4 on v3

--- a/solution.py
+++ b/solution.py
@@ -25,7 +25,15 @@
     return stages
 
 
+def joined_stages(stages):
+    (_, slabs, _), (_, size, _) = stages[:2]
+    return [("both", size * slabs, 1)] + stages[2:]
+
+
 def place(axis, size, stride):
+    if axis == "both":
+        slabs = lax.axis_size("space")
+        return lax.rem(lax.axis_index("dp"), size // slabs) * slabs + lax.axis_index("space")
     return lax.rem(lax.axis_index(axis) // stride, size)
 
 
@@ -35,6 +43,9 @@
     dp, space = lax.axis_index("dp"), lax.axis_index("space")
     if axis == "space":
         return other, (dp, other)
+    if axis == "both":
+        slabs = lax.axis_size("space")
+        return other, (dp + other // slabs - own // slabs, lax.rem(other, slabs))
     return other, (dp + (other - own) * stride, space)
 
 
@@ -48,6 +59,7 @@
         self.gathered, self.landing, self.sems = gathered, landing, sems
         self.start, self.length = 0, total.shape[0]
         self.starts, self.copies, self.sent, self.used = [], [], [], 0
+        self.done = 0
 
     def copy(self, source, target, device):
         send, recv = self.sems
@@ -103,6 +115,25 @@
             made.wait_recv()
         self.sent += self.copies
         self.copies = []
+
+    def step(self):
+        depth = len(self.stages)
+        index = self.done
+        self.done += 1
+        if index < depth:
+            self.scatter_finish(index)
+            if index + 1 < depth:
+                self.scatter_start(index + 1)
+                return
+            self.gather_own()
+            self.gather_start(depth - 1)
+            return
+        self.gather_finish()
+        if index + 1 < 2 * depth:
+            self.gather_start(2 * depth - 2 - index)
+
+    def pending(self):
+        return self.done < 2 * len(self.stages)
 
     def drain(self):
         for made in self.sent:
@@ -266,9 +297,11 @@
         del refs[:count]
         return taken
 
-    source_ref, cot_ref, mid_ref, deep_ref = take(4)
+    inputs = take(4)
     grad_in_ref, mid_out, deep_out = take(3)
-    mid_patches, deep_patches, deep_back, mid_back, mid_flip, deep_flip = take(6)
+    mid_patches, deep_patches, deep_back, mid_back, mid_flip, deep_flip, mid_turned, deep_turned = take(8)
+    held = take(4)
+    load_sem = take(1)[0]
     edges = [take(2) for _ in range(4)]
     edge_send, edge_recv = take(2)
     works = []
@@ -277,6 +310,10 @@
         landing = take(len(stages))
         works.append(Reduction(stages, total, outgoing, gathered, landing, take(2)))
     first, second, third = works
+    loads = [pltpu.make_async_copy(*pair, load_sem.at[at]) for at, pair in enumerate(zip(inputs, held))]
+    for load in loads:
+        load.start()
+    source_ref, cot_ref, mid_ref, deep_ref = held
     row_count, col_count = layout
     cells = row_count * col_count
     small = cells // 4
@@ -311,12 +348,10 @@
             one.wait_recv()
         fill_outer(patches, edges[index][1], low, high, row_count, col_count)
 
-    greet(plans[0])
+    greet(plans[2])
+    loads[0].wait()
     source = merged_planes(source_ref[...])
     swap0 = swap_start(0, source, cells)
-    for tap in range(27):
-        mid_flip[:, tap * chans2 : (tap + 1) * chans2] = mid_ref[(26 - tap) * chans1 : (27 - tap) * chans1]
-        deep_flip[:, tap * chans3 : (tap + 1) * chans3] = deep_ref[(26 - tap) * chans2 : (27 - tap) * chans2]
     deep_rows = deep_ref.shape[0]
     cut = deep_rows // 2
     half = mid_out.shape[0]
@@ -325,16 +360,21 @@
         if spare:
             work.total[used:] = jnp.zeros((spare, LANES), jnp.float32)
     fill_inner(mid_patches, source, row_count, col_count)
+    loads[2].wait()
+    mid_turned[...] = mid_ref[...].T
     swap_finish(0, swap0, mid_patches, row_count, col_count)
-    mid_pre = contract(mid_ref[...], mid_patches[...], 0, 0)
+    mid_pre = contract(mid_turned[...], mid_patches[...], 1, 0)
     mid_bend = gelu_bend(mid_pre)
     pooled = pool_cells(0.5 * mid_pre * (1.0 + mid_bend), row_count, col_count)
     swap1 = swap_start(1, pooled, small)
     fill_inner(deep_patches, pooled, row_count // 2, col_count // 2)
+    loads[3].wait()
+    deep_turned[...] = deep_ref[...].T
+    loads[1].wait()
     upstream = cot_ref[...].astype(jnp.float32).T
     mid_slope = gelu_slope(mid_pre, mid_bend)
     swap_finish(1, swap1, deep_patches, row_count // 2, col_count // 2)
-    deep_pre = contract(deep_ref[...], deep_patches[...], 0, 0)
+    deep_pre = contract(deep_turned[...], deep_patches[...], 1, 0)
     deep_grad = (upstream * gelu_slope(deep_pre, gelu_bend(deep_pre))).astype(jnp.bfloat16)
     swap2 = swap_start(2, deep_grad, small)
     first.total[:cut] = contract(deep_patches[:cut], deep_grad, 1, 1)
@@ -342,51 +382,32 @@
     second.total[: deep_rows - cut] = contract(deep_patches[cut:], deep_grad, 1, 1)
     second.scatter_start(0)
     fill_inner(deep_back, deep_grad, row_count // 2, col_count // 2)
+    for tap in range(27):
+        deep_flip[:, tap * chans3 : (tap + 1) * chans3] = deep_ref[(26 - tap) * chans2 : (27 - tap) * chans2]
     swap_finish(2, swap2, deep_back, row_count // 2, col_count // 2)
     back = contract(deep_flip[...], deep_back[...], 1, 0)
     mid_grad = (spread_cells(back, row_count, col_count) * 0.125 * mid_slope).astype(jnp.bfloat16)
     swap3 = swap_start(3, mid_grad, cells)
-    depth = len(plans[0])
-
-    def advance(work, index):
-        work.scatter_finish(index)
-        if index + 1 < depth:
-            work.scatter_start(index + 1)
-        else:
-            work.gather_own()
-            work.gather_start(depth - 1)
-
-    def collect(work, index):
-        work.gather_finish()
-        if index:
-            work.gather_start(index - 1)
-
-    advance(first, 0)
-    advance(second, 0)
+    first.step()
+    second.step()
     third.total[:half] = jnp.concatenate(
         [contract(mid_patches[:half], mid_grad, 1, 1), contract(mid_patches[half:], mid_grad, 1, 1)], axis=1
     )
     third.scatter_start(0)
-    advance(first, 1)
-    advance(second, 1)
+    first.step()
+    second.step()
     fill_inner(mid_back, mid_grad, row_count, col_count)
+    for tap in range(27):
+        mid_flip[:, tap * chans2 : (tap + 1) * chans2] = mid_ref[(26 - tap) * chans1 : (27 - tap) * chans1]
     swap_finish(3, swap3, mid_back, row_count, col_count)
-    advance(third, 0)
+    third.step()
     grad_in_ref[...] = contract(mid_flip[...], mid_back[...], 1, 0)
-    for index in range(2, depth):
-        advance(first, index)
-        advance(second, index)
-        advance(third, index - 1)
-    collect(first, depth - 1)
-    collect(second, depth - 1)
-    advance(third, depth - 1)
-    for index in reversed(range(depth - 1)):
-        collect(first, index)
-        collect(second, index)
-        collect(third, index + 1)
+    while any(work.pending() for work in works):
+        for work in works:
+            if work.pending():
+                work.step()
     deep_out[:cut] = first.gathered[:cut]
     deep_out[cut:] = second.gathered[: deep_rows - cut]
-    collect(third, 0)
     mid_out[...] = third.gathered[:half]
     for one in swap0 + swap1 + swap2 + swap3:
         one.wait_send()
@@ -397,7 +418,8 @@
 def shards(activations, cotangent, weight_mid, weight_deep):
     samples, slabs = lax.axis_size("dp"), lax.axis_size("space")
     stages = group_stages(samples, slabs)
-    plans = (stages, stages, stages)
+    turned = stages[:1] + stages[1:][::-1]
+    plans = (stages, turned, joined_stages(stages))
     chans1, chans2, chans3 = weight_mid.shape[3], weight_mid.shape[4], weight_deep.shape[4]
     source = activations[0]
     upstream = jnp.transpose(cotangent[0], (1, 2, 0)).reshape(-1, chans3)
@@ -414,6 +436,10 @@
         pltpu.VMEM((27 * chans2, cells), jnp.bfloat16),
         pltpu.VMEM((chans1, 27 * chans2), jnp.bfloat16),
         pltpu.VMEM((chans2, 27 * chans3), jnp.bfloat16),
+        pltpu.VMEM(mid_flat.shape[::-1], jnp.bfloat16),
+        pltpu.VMEM(deep_flat.shape[::-1], jnp.bfloat16),
+        *(pltpu.VMEM(one.shape, jnp.bfloat16) for one in (source, upstream, mid_flat, deep_flat)),
+        pltpu.SemaphoreType.DMA((4,)),
     ]
     for chans, width in ((chans1, plane), (chans2, small_plane), (chans3, small_plane), (chans2, plane)):
         scratch += [pltpu.VMEM((2, chans, width), jnp.bfloat16)] * 2
@@ -428,7 +454,7 @@
             jax.ShapeDtypeStruct((mid_flat.shape[0] // 2, LANES), jnp.bfloat16),
             jax.ShapeDtypeStruct(deep_flat.shape, jnp.bfloat16),
         ],
-        in_specs=[pl.BlockSpec(memory_space=pltpu.VMEM)] * 4,
+        in_specs=[pl.BlockSpec(memory_space=pltpu.HBM)] * 4,
         out_specs=[pl.BlockSpec(memory_space=pltpu.VMEM)] * 3,
         scratch_shapes=scratch,
         compiler_params=pltpu.CompilerParams(

time: 38.3 us -> 34.8 us (0.909)
  Pallas kernels: 33.8 us -> 30.3 us
    pallas_call x1, Pallas kernels: 32.6 us -> 29.1 us  [shards(): pl.pallas_call(functools.partial(block_kernel, plans, (ROWS, COLS)), out_...]
where the time goes in v4:
time: 34.8 us; the launch traced here: 34.5 us
  Pallas kernels  30.3 us (87%)
  local copies, waits for them, and re-layouts  3.54 us (10%)
  between operations  0.65 us (2%)
    pallas_call x1, Pallas kernels, shards(): pl.pallas_call(functools.partial(block_kernel, plans, (ROWS, COLS)), out_...  29.1 us
    unnamed x8, local copies, waits for them, and re-layouts  3.54 us
    pallas_call x1, Pallas kernels, shards(): pl.pallas_call(functools.partial(finish_kernel, 1.0 / samples), out_shape...  1.21 us

profile of v4, /device:TPU:1, one launch (start us, length us, event | category | flops | bytes accessed | tf_op | source)
XLA Modules:
  0.0 34.5 jit_solution(6035403837057383834)
XLA Ops:
  0.6 0.0 copy-start
  0.6 1.0 %copy-done = bf16[3,3,3,64,128]{4,3,2,1,0:T(8,128)(2,1)S(1)} copy-done((bf16[3,3,3,64,128]{4,3,2,1,0:T(8,128)(2,1)S(1)}, bf16[3,3,3,64,128]{4,3,2,1,0:T(8,128)(2,1)}, u32[]{:S(2)}) %copy-start) | copy-done | bytes 442392
  1.6 0.0 copy-start.1
  1.6 0.9 %copy-done.1 = bf16[3,3,3,32,64]{4,3,2,1,0:T(8,128)(2,1)S(1)} copy-done((bf16[3,3,3,32,64]{4,3,2,1,0:T(8,128)(2,1)S(1)}, bf16[3,3,3,32,64]{4,3,2,1,0:T(8,128)(2,1)}, u32[]{:S(2)}) %copy-start.1) | copy-done | bytes 110616
  2.6 0.0 copy-start.2
  2.6 0.8 %copy-done.2 = bf16[1,32,4,256]{3,2,1,0:T(4,128)(2,1)S(1)} copy-done((bf16[1,32,4,256]{3,2,1,0:T(4,128)(2,1)S(1)}, bf16[1,32,4,256]{3,2,1,0:T(4,128)(2,1)}, u32[]{:S(2)}) %copy-start.2) | copy-done | bytes 65560
  3.4 0.0 copy-start.3
  3.4 0.8 %copy-done.3 = bf16[1,128,2,64]{1,3,2,0:T(8,128)(2,1)S(1)} copy-done((bf16[1,128,2,64]{1,3,2,0:T(8,128)(2,1)S(1)}, bf16[1,128,2,64]{1,3,2,0:T(8,128)(2,1)}, u32[]{:S(2)}) %copy-start.3) | copy-done | bytes 32792
  4.2 29.1 %shard_map.67 = (f32[32,1024]{1,0:T(8,128)S(1)}, bf16[432,128]{1,0:T(8,128)(2,1)S(1)}, bf16[1728,128]{1,0:T(8,128)(2,1)S(1)}) custom-call(bf16[32,4,256]{2,1,0:T(4,128)(2,1)S(1)} %bitcast.13, bf16[128,128]{1,0:T(8,128)(2,1)S(1)} %bitcast.14, bf16[864,64]{1,0:T(8,128)(2,1)S(1)} %bitcast.12, bf16[1728,128]{1,0:T(8,128)(2,1)S(1)} %bitcast.11), custom_call_target="tpu_custom_call" | custom-call | tf_op jit(solution)/shard_map/pallas_call | solution.py:450
  33.3 1.2 %shard_map.68 = (bf16[32,4,256]{2,1,0:T(4,128)(2,1)}, f32[864,64]{1,0:T(8,128)}, f32[1728,128]{1,0:T(8,128)}) custom-call(f32[32,1024]{1,0:T(8,128)S(1)} %get-tuple-element.9.grad_in_ref, bf16[432,128]{1,0:T(8,128)(2,1)S(1)} %get-tuple-element.10.mid_ref, bf16[1728,128]{1,0:T(8,128)(2,1)S(1)} %get-tuple-element.11.deep_ref), custom_call_target="tpu_custom_call" | custom-call | tf_op jit(solution)/shard_map/pallas_call | solution.py:464
Async XLA Ops:
  0.6 1.0 %copy-start = (bf16[3,3,3,64,128]{4,3,2,1,0:T(8,128)(2,1)S(1)}, bf16[3,3,3,64,128]{4,3,2,1,0:T(8,128)(2,1)}, u32[]{:S(2)}) copy-start(bf16[3,3,3,64,128]{4,3,2,1,0:T(8,128)(2,1)} %param.7) | copy-start | bytes 1327108
  1.6 0.9 %copy-start.1 = (bf16[3,3,3,32,64]{4,3,2,1,0:T(8,128)(2,1)S(1)}, bf16[3,3,3,32,64]{4,3,2,1,0:T(8,128)(2,1)}, u32[]{:S(2)}) copy-start(bf16[3,3,3,32,64]{4,3,2,1,0:T(8,128)(2,1)} %param.6) | copy-start | bytes 331780
  2.6 0.8 %copy-start.2 = (bf16[1,32,4,256]{3,2,1,0:T(4,128)(2,1)S(1)}, bf16[1,32,4,256]{3,2,1,0:T(4,128)(2,1)}, u32[]{:S(2)}) copy-start(bf16[1,32,4,256]{3,2,1,0:T(4,128)(2,1)} %param.4) | copy-start | bytes 196612
  3.4 0.8 %copy-start.3 = (bf16[1,128,2,64]{1,3,2,0:T(8,128)(2,1)S(1)}, bf16[1,128,2,64]{1,3,2,0:T(8,128)(2,1)}, u32[]{:S(2)}) copy-start(bf16[1,128,2,64]{1,3,2,0:T(8,128)(2,1)} %param.5) | copy-start | bytes 98308

commit v5 on v4

--- a/solution.py
+++ b/solution.py
@@ -166,7 +166,7 @@
             _, device = partner(axis, size, stride, step)
             pl.semaphore_signal(barrier, inc=1, device_id=device, device_id_type=pl.DeviceIdType.MESH)
             count += 1
-    pl.semaphore_wait(barrier, count)
+    return count
 
 
 def moved_planes(planes, row_tap, col_tap, row_count, col_count):
@@ -326,8 +326,9 @@
 
     def swap_start(index, planes, cells_here):
         leaving, arriving = edges[index]
-        leaving[0] = planes[:, :cells_here]
-        leaving[1] = planes[:, planes.shape[1] - cells_here :]
+        if planes is not None:
+            leaving[0] = planes[:, :cells_here]
+            leaving[1] = planes[:, planes.shape[1] - cells_here :]
         made = []
         for side, other in ((0, lax.rem(space + slabs - 1, slabs)), (1, lax.rem(space + 1, slabs))):
             made.append(
@@ -348,10 +349,13 @@
             one.wait_recv()
         fill_outer(patches, edges[index][1], low, high, row_count, col_count)
 
-    greet(plans[2])
+    greeted = greet(plans[2])
     loads[0].wait()
     source = merged_planes(source_ref[...])
-    swap0 = swap_start(0, source, cells)
+    edges[0][0][0] = source[:, :cells]
+    edges[0][0][1] = source[:, source.shape[1] - cells :]
+    pl.semaphore_wait(pltpu.get_barrier_semaphore(), greeted)
+    swap0 = swap_start(0, None, cells)
     deep_rows = deep_ref.shape[0]
     cut = deep_rows // 2
     half = mid_out.shape[0]
@@ -394,9 +398,9 @@
         [contract(mid_patches[:half], mid_grad, 1, 1), contract(mid_patches[half:], mid_grad, 1, 1)], axis=1
     )
     third.scatter_start(0)
+    fill_inner(mid_back, mid_grad, row_count, col_count)
     first.step()
     second.step()
-    fill_inner(mid_back, mid_grad, row_count, col_count)
     for tap in range(27):
         mid_flip[:, tap * chans2 : (tap + 1) * chans2] = mid_ref[(26 - tap) * chans1 : (27 - tap) * chans1]
     swap_finish(3, swap3, mid_back, row_count, col_count)
@@ -446,7 +450,6 @@
     scratch += [pltpu.SemaphoreType.DMA((8,)), pltpu.SemaphoreType.DMA((8,))]
     for plan, rows in zip(plans, (half_rows, half_rows, mid_rows)):
         scratch += reduction_scratch(plan, rows)
-    room = 24 * 1024 * 1024 + 12 * LANES * (2 * half_rows + mid_rows)
     grad_in, mid_sum, deep_sum = pl.pallas_call(
         functools.partial(block_kernel, plans, (ROWS, COLS)),
         out_shape=[
@@ -458,7 +461,7 @@
         out_specs=[pl.BlockSpec(memory_space=pltpu.VMEM)] * 3,
         scratch_shapes=scratch,
         compiler_params=pltpu.CompilerParams(
-            collective_id=0, has_side_effects=True, vmem_limit_bytes=min(room, 56 * 1024 * 1024)
+            collective_id=0, has_side_effects=True, vmem_limit_bytes=56 * 1024 * 1024
         ),
     )(source, upstream, mid_flat, deep_flat)
     grad_in, mid_sum, deep_sum = pl.pallas_call(
@@ -470,7 +473,7 @@
         ],
         in_specs=[pl.BlockSpec(memory_space=pltpu.VMEM)] * 3,
         out_specs=[pl.BlockSpec(memory_space=pltpu.VMEM)] * 3,
-        compiler_params=pltpu.CompilerParams(vmem_limit_bytes=16 * 1024 * 1024),
+        compiler_params=pltpu.CompilerParams(vmem_limit_bytes=56 * 1024 * 1024),
     )(grad_in, mid_sum, deep_sum)
     return (
         grad_in.reshape(activations.shape),

time: 34.8 us -> 32.4 us (0.931)
  local copies, waits for them, and re-layouts: 3.54 us -> 0 us
  Pallas kernels: 30.3 us -> 31.6 us
    unnamed x8 -> x0, local copies, waits for them, and re-layouts: 3.54 us -> none
    pallas_call x1, Pallas kernels: 1.21 us -> 2.35 us  [shards(): pl.pallas_call(functools.partial(finish_kernel, 1.0 / samples), out_shape...]
where the time goes in v5:
time: 32.4 us; the launch traced here: 32.2 us
  Pallas kernels  31.6 us (98%)
  between operations  0.64 us (2%)
    pallas_call x1, Pallas kernels, shards(): pl.pallas_call(functools.partial(block_kernel, plans, (ROWS, COLS)), out_...  29.2 us
    pallas_call x1, Pallas kernels, shards(): pl.pallas_call(functools.partial(finish_kernel, 1.0 / samples), out_shape...  2.35 us

profile of v5, /device:TPU:1, one launch (start us, length us, event | category | flops | bytes accessed | tf_op | source)
XLA Modules:
  0.0 32.2 jit_solution(6257642114876643717)
XLA Ops:
  0.6 29.2 %shard_map.67 = (f32[32,1024]{1,0:T(8,128)}, bf16[432,128]{1,0:T(8,128)(2,1)}, bf16[1728,128]{1,0:T(8,128)(2,1)}) custom-call(bf16[32,4,256]{2,1,0:T(4,128)(2,1)} %bitcast.13, bf16[128,128]{1,0:T(8,128)(2,1)} %bitcast.14, bf16[864,64]{1,0:T(8,128)(2,1)} %bitcast.12, bf16[1728,128]{1,0:T(8,128)(2,1)} %bitcast.11), custom_call_target="tpu_custom_call" | custom-call | tf_op jit(solution)/shard_map/pallas_call | solution.py:453
  29.9 2.4 %shard_map.68 = (bf16[32,4,256]{2,1,0:T(4,128)(2,1)}, f32[864,64]{1,0:T(8,128)}, f32[1728,128]{1,0:T(8,128)}) custom-call(f32[32,1024]{1,0:T(8,128)} %get-tuple-element.9.grad_in_ref, bf16[432,128]{1,0:T(8,128)(2,1)} %get-tuple-element.10.mid_ref, bf16[1728,128]{1,0:T(8,128)(2,1)} %get-tuple-element.11.deep_ref), custom_call_target="tpu_custom_call" | custom-call | tf_op jit(solution)/shard_map/pallas_call | solution.py:467

commit v6 on v5

--- a/solution.py
+++ b/solution.py
@@ -301,7 +301,7 @@
     grad_in_ref, mid_out, deep_out = take(3)
     mid_patches, deep_patches, deep_back, mid_back, mid_flip, deep_flip, mid_turned, deep_turned = take(8)
     held = take(4)
-    load_sem = take(1)[0]
+    load_sem, store_sem, grad_held = take(3)
     edges = [take(2) for _ in range(4)]
     edge_send, edge_recv = take(2)
     works = []
@@ -405,14 +405,22 @@
         mid_flip[:, tap * chans2 : (tap + 1) * chans2] = mid_ref[(26 - tap) * chans1 : (27 - tap) * chans1]
     swap_finish(3, swap3, mid_back, row_count, col_count)
     third.step()
-    grad_in_ref[...] = contract(mid_flip[...], mid_back[...], 1, 0)
+    grad_held[...] = contract(mid_flip[...], mid_back[...], 1, 0)
+    stores = [pltpu.make_async_copy(grad_held, grad_in_ref, store_sem.at[0])]
+    stores[0].start()
     while any(work.pending() for work in works):
         for work in works:
             if work.pending():
                 work.step()
-    deep_out[:cut] = first.gathered[:cut]
-    deep_out[cut:] = second.gathered[: deep_rows - cut]
-    mid_out[...] = third.gathered[:half]
+    for source, target in (
+        (first.gathered.at[:cut], deep_out.at[:cut]),
+        (second.gathered.at[: deep_rows - cut], deep_out.at[cut:]),
+        (third.gathered.at[:half], mid_out),
+    ):
+        stores.append(pltpu.make_async_copy(source, target, store_sem.at[len(stores)]))
+        stores[-1].start()
+    for one in stores:
+        one.wait()
     for one in swap0 + swap1 + swap2 + swap3:
         one.wait_send()
     for work in works:
@@ -444,6 +452,8 @@
         pltpu.VMEM(deep_flat.shape[::-1], jnp.bfloat16),
         *(pltpu.VMEM(one.shape, jnp.bfloat16) for one in (source, upstream, mid_flat, deep_flat)),
         pltpu.SemaphoreType.DMA((4,)),
+        pltpu.SemaphoreType.DMA((4,)),
+        pltpu.VMEM((chans1, cells), jnp.float32),
     ]
     for chans, width in ((chans1, plane), (chans2, small_plane), (chans3, small_plane), (chans2, plane)):
         scratch += [pltpu.VMEM((2, chans, width), jnp.bfloat16)] * 2
@@ -458,7 +468,7 @@
             jax.ShapeDtypeStruct(deep_flat.shape, jnp.bfloat16),
         ],
         in_specs=[pl.BlockSpec(memory_space=pltpu.HBM)] * 4,
-        out_specs=[pl.BlockSpec(memory_space=pltpu.VMEM)] * 3,
+        out_specs=[pl.BlockSpec(memory_space=pltpu.HBM)] * 3,
         scratch_shapes=scratch,
         compiler_params=pltpu.CompilerParams(
             collective_id=0, has_side_effects=True, vmem_limit_bytes=56 * 1024 * 1024

time: 32.4 us -> 32.3 us (level)
  no operation moved by 1% of the time
where the time goes in v6:
time: 32.3 us; the launch traced here: 32.1 us
  Pallas kernels  31.5 us (98%)
  between operations  0.64 us (2%)
    pallas_call x1, Pallas kernels, shards(): pl.pallas_call(functools.partial(block_kernel, plans, (ROWS, COLS)), out_...  29.2 us
    pallas_call x1, Pallas kernels, shards(): pl.pallas_call(functools.partial(finish_kernel, 1.0 / samples), out_shape...  2.35 us

profile of v6, /device:TPU:1, one launch (start us, length us, event | category | flops | bytes accessed | tf_op | source)
XLA Modules:
  0.0 32.1 jit_solution(5382634747895667494)
XLA Ops:
  0.6 29.2 %shard_map.67 = (f32[32,1024]{1,0:T(8,128)}, bf16[432,128]{1,0:T(8,128)(2,1)}, bf16[1728,128]{1,0:T(8,128)(2,1)}) custom-call(bf16[32,4,256]{2,1,0:T(4,128)(2,1)} %bitcast.13, bf16[128,128]{1,0:T(8,128)(2,1)} %bitcast.14, bf16[864,64]{1,0:T(8,128)(2,1)} %bitcast.12, bf16[1728,128]{1,0:T(8,128)(2,1)} %bitcast.11), custom_call_target="tpu_custom_call" | custom-call | tf_op jit(solution)/shard_map/pallas_call | solution.py:463
  29.8 2.4 %shard_map.68 = (bf16[32,4,256]{2,1,0:T(4,128)(2,1)}, f32[864,64]{1,0:T(8,128)}, f32[1728,128]{1,0:T(8,128)}) custom-call(f32[32,1024]{1,0:T(8,128)} %get-tuple-element.9.grad_in_ref, bf16[432,128]{1,0:T(8,128)(2,1)} %get-tuple-element.10.mid_ref, bf16[1728,128]{1,0:T(8,128)(2,1)} %get-tuple-element.11.deep_ref), custom_call_target="tpu_custom_call" | custom-call | tf_op jit(solution)/shard_map/pallas_call | solution.py:477
